TPU v7x, 128 devices: a whole 4x4x4 slice. The times are simulated.
128 devices in a mesh: stretch: 32 (over x, y, core), section: 4 (over z).
Axes of the slice: x: 4, y: 4, z: 4, core: 2. Of those that a mesh axis runs over, the one named last changes fastest.
Arguments:
- latents: bfloat16 [4096, 3072], P('stretch'), may hold values from -6 to 6
- noise_levels: int32 [32], replicated, may hold values from 0 to 15
- frame_lengths: int32 [32], replicated, may hold values from 32 to 128, as said below
- kv_weight: bfloat16 [4, 3072, 1024], P('section'), may hold values from -2 to 2
- mod_shift: float32 [4, 16, 3072], P('section'), may hold values from -3 to 3
- mod_scale: float32 [4, 16, 3072], P('section'), may hold values from -0.5 to 0.5
- mod_gate: float32 [4, 16, 3072], P('section'), may hold values from 0.5 to 2
Outputs:
- hidden: bfloat16 [4, 4096, 3072], P('section', 'stretch')
Inputs may be any that keep to these rules, and one draw needn't show every extreme that they name: `frame_lengths`: some video block has all 128 tokens valid.
All inputs are finite; a program needn't handle non-finite values.
Results may differ from a plain program's by a relative error of at most 0.017.
Values may be sent and summed in bfloat16 or wider, within the bound.
A program may use at most 192 MiB of HBM per device.

v0:
```python
import math

import jax
import jax.numpy as jnp
from jax import lax
from jax.sharding import PartitionSpec as P

HEAD = 128


def passed_along(block, axis, distance):
    devices = range(lax.axis_size(axis))
    route = [(i - distance, i) for i in devices if i - distance in devices]
    return lax.ppermute(block, axis, route)


def modulate(current, shift_row, scale_row):
    floats = current.astype(jnp.float32)
    row_mean = jnp.mean(floats, axis=-1, keepdims=True)
    row_var = jnp.mean((floats - row_mean) ** 2, axis=-1, keepdims=True)
    unit = (floats - row_mean) * lax.rsqrt(row_var + 1e-06)
    normed = (unit * (1.0 + scale_row) + shift_row).astype(jnp.bfloat16)
    return (floats, normed)


def shards(latents, noise_levels, frame_lengths, kv_weight, mod_shift, mod_scale, mod_gate):
    tok_rows, model_width = latents.shape
    block_id = lax.axis_index("stretch")
    section_id = lax.axis_index("section")
    sections = lax.axis_size("section")
    block_count = noise_levels.shape[0]
    kv_width = kv_weight.shape[2] // 2
    kv_heads = kv_width // HEAD
    head_group = model_width // HEAD // kv_heads
    block_ids = jnp.arange(block_count, dtype=jnp.int32)
    block_level = jnp.sum(jnp.where(block_ids == block_id, noise_levels, 0))
    level_pick = jnp.arange(mod_shift.shape[1], dtype=jnp.int32) == block_level

    def row_of(table):
        return jnp.sum(jnp.where(level_pick[:, None], table[0], 0.0), axis=0)

    shift_row = row_of(mod_shift)
    scale_row = row_of(mod_scale)
    gate_row = row_of(mod_gate)

    def key_mask(count):
        positions = jnp.arange(count, dtype=jnp.int32)
        key_owner = positions // tok_rows
        within = positions % tok_rows
        key_lengths = jnp.sum(
            jnp.where(key_owner[:, None] == block_ids[None, :], frame_lengths[None, :], 0), axis=1
        )
        return (key_owner <= block_id) & (within < key_lengths)

    def attend(queries, kv_local, active):
        local_heads = queries.shape[1]
        key_span = local_heads * HEAD
        out_shape = (tok_rows, local_heads, head_group, HEAD)

        def head_scores(partial_kv, head_idx):
            key_head = partial_kv[:, head_idx * HEAD : (head_idx + 1) * HEAD]
            return jnp.einsum(
                "tgd,sd->gts", queries[:, head_idx], key_head, preferred_element_type=jnp.float32
            ) / math.sqrt(HEAD)

        def head_values(partial_kv, head_idx):
            return partial_kv[
                :, key_span + head_idx * HEAD : key_span + (head_idx + 1) * HEAD
            ].astype(jnp.float32)

        kv_all = lax.all_gather(kv_local, "stretch", axis=0, tiled=True)

        def full_attend(gathered):
            allowed = key_mask(gathered.shape[0])
            head_outs = []
            for head_idx in range(local_heads):
                masked = jnp.where(allowed, head_scores(gathered, head_idx), -1e30)
                row_top = jnp.max(masked, axis=-1, keepdims=True)
                expons = jnp.where(allowed, jnp.exp(masked - row_top), 0.0)
                weights = expons / jnp.sum(expons, axis=-1, keepdims=True)
                head_outs.append(
                    jnp.einsum(
                        "gts,sd->tgd",
                        weights,
                        head_values(gathered, head_idx),
                        precision=lax.Precision.HIGHEST,
                    )
                )
            return jnp.stack(head_outs, axis=1)

        def no_attend(gathered):
            return jnp.zeros(out_shape, jnp.float32)

        return lax.cond(active, full_attend, no_attend, kv_all)

    weight = kv_weight[0]

    def prepare(current):
        floats, normed = modulate(current, shift_row, scale_row)
        kv_local = jnp.dot(normed, weight, preferred_element_type=jnp.float32).astype(jnp.bfloat16)
        return (floats, normed, kv_local)

    def bypass(current):
        return (
            jnp.zeros((tok_rows, model_width), jnp.float32),
            jnp.zeros((tok_rows, model_width), jnp.bfloat16),
            jnp.zeros((tok_rows, 2 * kv_width), jnp.bfloat16),
        )

    def step_body(step_idx, loop_state):
        current, result = loop_state
        active = section_id == step_idx
        floats, normed, kv_local = lax.cond(active, prepare, bypass, current)
        queries = normed.reshape(tok_rows, kv_heads, head_group, HEAD)
        attended = attend(queries, kv_local, active).reshape(tok_rows, model_width)
        produced = (floats + gate_row * attended).astype(jnp.bfloat16)
        result = jnp.where(active, produced, result)
        handed = passed_along(produced, "section", 1)
        current = jnp.where(section_id == 0, latents, handed)
        return (current, result)

    final_input, result = lax.fori_loop(0, sections, step_body, (latents, jnp.zeros_like(latents)))
    return result[None]


def solution(mesh):
    in_specs = (
        P("stretch", None),
        P(),
        P(),
        P("section", None, None),
        P("section", None, None),
        P("section", None, None),
        P("section", None, None),
    )
    out_specs = P("section", "stretch", None)
    return jax.shard_map(shards, mesh=mesh, in_specs=in_specs, out_specs=out_specs, check_vma=False)
```

profile of v0, /device:TPU:96, one launch (start us, length us, event | category | flops | bytes accessed | tf_op | source)
XLA Modules:
  0.0 760.3 jit_solution(8332196079190259105)
XLA Ops:
  6.5 1.3 fusion.134
  8.5 1.9 fusion.131
  10.4 2.3 copy.43
  12.7 1.1 copy.59
  13.8 738.3 %while.17 = (s32[]{:T(128)}, bf16[128,3072]{0,1:T(8,128)(2,1)S(1)}, bf16[128,3072]{0,1:T(8,128)(2,1)S(1)}, pred[]{:T(512)}, s32[]{:T(128)}, /*index=5*/f32[3072]...) while((s32[]{:T(128)}, bf16[128,3072]{0,1:T(8,128)(2,1)S(1)}, ...), condition=%wide.region_20.21_spmd.clone, body=%wide.region_4.20_spmd.clone.sunk | while | flops 23437488128 | bytes 183957280 | solution.py:122
  13.8 2.4 conditional.6
  13.8 1.3 broadcast.108
  15.1 1.0 reshape.62
  16.2 0.7 copy-done
  16.9 58.9 %all-gather.2.cloned.1.call-done = bf16[4096,1024]{1,0:T(8,128)(2,1)} async-done(((bf16[128,1024]{1,0:T(8,128)(2,1)}), bf16[4096,1024]{1,0:T(8,128)(2,1)}) %all-gather.2.cloned.1.call-update) | async-done | bytes 8388624 | tf_op jit(solution)/shard_map/while/body/eval_jaxpr/all_gather | solution.py:71
  76.1 3.2 select_select_fusion.2
  79.3 1.3 collective-permute-start
  80.6 21.2 %collective-permute-done = bf16[128,3072]{0,1:T(8,128)(2,1)S(1)} collective-permute-done((bf16[128,3072]{0,1:T(8,128)(2,1)S(1)}, bf16[128,3072]{0,1:T(8,128)(2,1)S(1)}, u32[]{:S(2)}, u32[]{:S(2)}) %collective-permute-start) | collective-permute-done | bytes 786464 | tf_op jit(solution)/shard_map/while/body/eval_jaxpr/ppermute | solution.py:14
  102.2 2.4 conditional.6
  102.2 1.3 broadcast.108
  103.5 1.0 reshape.62
  105.3 153.4 %all-gather.2.cloned.1.call-done = bf16[4096,1024]{1,0:T(8,128)(2,1)} async-done(((bf16[128,1024]{1,0:T(8,128)(2,1)}), bf16[4096,1024]{1,0:T(8,128)(2,1)}) %all-gather.2.cloned.1.call-update) | async-done | bytes 8388624 | tf_op jit(solution)/shard_map/while/body/eval_jaxpr/all_gather | solution.py:71
  259.0 3.2 select_select_fusion.2
  262.2 1.3 collective-permute-start
  263.5 20.3 %collective-permute-done = bf16[128,3072]{0,1:T(8,128)(2,1)S(1)} collective-permute-done((bf16[128,3072]{0,1:T(8,128)(2,1)S(1)}, bf16[128,3072]{0,1:T(8,128)(2,1)S(1)}, u32[]{:S(2)}, u32[]{:S(2)}) %collective-permute-start) | collective-permute-done | bytes 786464 | tf_op jit(solution)/shard_map/while/body/eval_jaxpr/ppermute | solution.py:14
  284.1 2.4 conditional.6
  284.2 1.3 broadcast.108
  285.5 1.0 reshape.62
  287.2 156.4 %all-gather.2.cloned.1.call-done = bf16[4096,1024]{1,0:T(8,128)(2,1)} async-done(((bf16[128,1024]{1,0:T(8,128)(2,1)}), bf16[4096,1024]{1,0:T(8,128)(2,1)}) %all-gather.2.cloned.1.call-update) | async-done | bytes 8388624 | tf_op jit(solution)/shard_map/while/body/eval_jaxpr/all_gather | solution.py:71
  443.9 3.2 select_select_fusion.2
  447.1 1.3 collective-permute-start
  448.4 116.5 %collective-permute-done = bf16[128,3072]{0,1:T(8,128)(2,1)S(1)} collective-permute-done((bf16[128,3072]{0,1:T(8,128)(2,1)S(1)}, bf16[128,3072]{0,1:T(8,128)(2,1)S(1)}, u32[]{:S(2)}, u32[]{:S(2)}) %collective-permute-start) | collective-permute-done | bytes 786464 | tf_op jit(solution)/shard_map/while/body/eval_jaxpr/ppermute | solution.py:14
  565.3 10.3 %conditional.6 = (f32[128,3072]{0,1:T(8,128)}, bf16[128,1024]{1,0:T(8,128)(2,1)S(1)}, bf16[128,4,6,128]{0,3,2,1:T(8,128)(2,1)}) conditional(s32[]{:T(128)} %convert_element_type.38, () %tuple.79, (bf16[128,3072]{0,1:T(8,128)(2,1)S(1)}, f32[3072]{0:T(1024)}, f32[3072]{0:T(1024)S(1)}, bf16[3072,1024]{1,0:T(8,128)(2,1)}) %tuple.80), branch_computations={%region_5.5_spmd, %region_6.8_spmd} | conditional | flops 809372800 | bytes 12898844 | solution.py:113
  565.8 1.5 multiply_reduce_fusion
  567.3 0.7 broadcast_add_fusion
  568.0 3.5 add_convert_fusion
  571.5 4.1 convolution_convert_fusion
  576.3 52.3 %all-gather.2.cloned.1.call-done = bf16[4096,1024]{1,0:T(8,128)(2,1)} async-done(((bf16[128,1024]{1,0:T(8,128)(2,1)}), bf16[4096,1024]{1,0:T(8,128)(2,1)}) %all-gather.2.cloned.1.call-update) | async-done | bytes 8388624 | tf_op jit(solution)/shard_map/while/body/eval_jaxpr/all_gather | solution.py:71
  628.7 97.2 %conditional.7 = (f32[128,3072]{0,1:T(8,128)S(1)}) conditional(s32[]{:T(128)} %convert_element_type.38, () %tuple.81, (s32[]{:T(128)}, s32[32]{0:T(128)S(1)}, s32[32]{0:T(128)S(1)}, bf16[4096,1024]{1,0:T(8,128)(2,1)}, bf16[128,4,6,128]{0,3,2,1:T(8,128)(2,1)}) %tuple.93), branch_computations={%region_9.9_spmd, %region_10.19_spmd} | conditional | flops 22625755136 | bytes 133034248 | solution.py:94
  628.7 1.5 copy.42
  630.4 11.1 %fusion.150 = (f32[6,128]{1,0:T(8,128)S(1)}, f32[6,128,4096]{1,2,0:T(8,128)}) fusion(pred[4096]{0:T(1024)(128)(4,1)S(1)} %fusion.122, bf16[4096,1024]{1,0:T(8,128)(2,1)} %get-tuple-element.277, bf16[128,4,6,128]{3,0,2,1:T(8,128)(2,1)S(1)} %copy.42), kind=kOutput, calls=%fused_computation.133 | convolution fusion | flops 821039104 | bytes 13839360 | tf_op jit(solution)/shard_map/while/body/eval_jaxpr/cond/branch_1_fun/sub | solution.py:79
  641.5 11.3 %copy.34 = bf16[4096,1024]{0,1:T(8,128)(2,1)} copy(bf16[4096,1024]{1,0:T(8,128)(2,1)} %get-tuple-element.277) | data formatting | bytes 16777216 | tf_op jit(solution)/shard_map
  652.8 9.7 %fusion.58 = f32[128,1,6,128]{0,3,2,1:T(8,128)S(1)} fusion(f32[6,128,4096]{1,2,0:T(8,128)} %get-tuple-element.435, f32[6,128]{1,0:T(8,128)S(1)} %get-tuple-element.434, bf16[4096,1024]{0,1:T(8,128)(2,1)} %copy.34), kind=kOutput, calls=%fused_computation.64 | convolution fusion | flops 4834983936 | bytes 14027776 | tf_op jit(solution)/shard_map/while/body/eval_jaxpr/cond/branch_1_fun/gts,sd->tgd/dot_general | solution.py:82
  662.6 11.1 %fusion.145 = (f32[6,128]{1,0:T(8,128)S(1)}, f32[6,128,4096]{1,2,0:T(8,128)}) fusion(pred[4096]{0:T(1024)(128)(4,1)S(1)} %fusion.122, bf16[4096,1024]{1,0:T(8,128)(2,1)} %get-tuple-element.277, bf16[128,4,6,128]{3,0,2,1:T(8,128)(2,1)S(1)} %copy.42), kind=kOutput, calls=%fused_computation.132 | convolution fusion | flops 821039104 | bytes 13839360 | tf_op jit(solution)/shard_map/while/body/eval_jaxpr/cond/branch_1_fun/sub | solution.py:79
  673.7 9.9 %fusion.61 = f32[128,1,6,128]{0,3,2,1:T(8,128)S(1)} fusion(f32[6,128,4096]{1,2,0:T(8,128)} %get-tuple-element.433, f32[6,128]{1,0:T(8,128)S(1)} %get-tuple-element.432, bf16[4096,1024]{0,1:T(8,128)(2,1)} %copy.34), kind=kOutput, calls=%fused_computation.65 | convolution fusion | flops 4834983936 | bytes 14027776 | tf_op jit(solution)/shard_map/while/body/eval_jaxpr/cond/branch_1_fun/gts,sd->tgd/dot_general | solution.py:82
  683.6 11.1 %fusion.140 = (f32[6,128]{1,0:T(8,128)S(1)}, f32[6,128,4096]{1,2,0:T(8,128)}) fusion(pred[4096]{0:T(1024)(128)(4,1)S(1)} %fusion.122, bf16[4096,1024]{1,0:T(8,128)(2,1)} %get-tuple-element.277, bf16[128,4,6,128]{3,0,2,1:T(8,128)(2,1)S(1)} %copy.42), kind=kOutput, calls=%fused_computation.131 | convolution fusion | flops 821039104 | bytes 13839360 | tf_op jit(solution)/shard_map/while/body/eval_jaxpr/cond/branch_1_fun/sub | solution.py:79
  694.7 9.9 %fusion.64 = f32[128,1,6,128]{0,3,2,1:T(8,128)S(1)} fusion(f32[6,128,4096]{1,2,0:T(8,128)} %get-tuple-element.431, f32[6,128]{1,0:T(8,128)S(1)} %get-tuple-element.430, bf16[4096,1024]{0,1:T(8,128)(2,1)} %copy.34), kind=kOutput, calls=%fused_computation.66 | convolution fusion | flops 4834983936 | bytes 14027776 | tf_op jit(solution)/shard_map/while/body/eval_jaxpr/cond/branch_1_fun/gts,sd->tgd/dot_general | solution.py:82
  704.6 11.1 %fusion.135 = (f32[6,128]{1,0:T(8,128)S(1)}, f32[6,128,4096]{1,2,0:T(8,128)}) fusion(pred[4096]{0:T(1024)(128)(4,1)S(1)} %fusion.122, bf16[4096,1024]{1,0:T(8,128)(2,1)} %get-tuple-element.277, bf16[128,4,6,128]{3,0,2,1:T(8,128)(2,1)S(1)} %copy.42), kind=kOutput, calls=%fused_computation.130 | convolution fusion | flops 821039104 | bytes 13839360 | tf_op jit(solution)/shard_map/while/body/eval_jaxpr/cond/branch_1_fun/sub | solution.py:79
  715.7 9.7 %fusion.67 = f32[128,1,6,128]{0,3,2,1:T(8,128)S(1)} fusion(f32[6,128,4096]{1,2,0:T(8,128)} %get-tuple-element.429, f32[6,128]{1,0:T(8,128)S(1)} %get-tuple-element.428, bf16[4096,1024]{0,1:T(8,128)(2,1)} %copy.34), kind=kOutput, calls=%fused_computation.67 | convolution fusion | flops 4834983936 | bytes 14027776 | tf_op jit(solution)/shard_map/while/body/eval_jaxpr/cond/branch_1_fun/gts,sd->tgd/dot_general | solution.py:82
  725.8 3.2 select_select_fusion.2
  729.0 1.3 collective-permute-start
  730.3 20.3 %collective-permute-done = bf16[128,3072]{0,1:T(8,128)(2,1)S(1)} collective-permute-done((bf16[128,3072]{0,1:T(8,128)(2,1)S(1)}, bf16[128,3072]{0,1:T(8,128)(2,1)S(1)}, u32[]{:S(2)}, u32[]{:S(2)}) %collective-permute-start) | collective-permute-done | bytes 786464 | tf_op jit(solution)/shard_map/while/body/eval_jaxpr/ppermute | solution.py:14
  752.1 1.2 copy.45
  (49 shorter events, 5.2 us)
Async XLA Ops:
  13.8 62.0 %copy-start.1 = (s32[32]{0:T(128)S(1)}, s32[32]{0:T(128)}, u32[]{:S(2)}) copy-start(s32[32]{0:T(128)} %get-tuple-element.563) | copy-start | bytes 388 | tf_op jit(solution)/shard_map/while
  13.8 62.0 %all-gather.2.cloned.1.call-start = ((), (), s32[]{:S(2)}) async-start(), calls=%async_computation | async-start | bytes 8650752 | tf_op jit(solution)/shard_map/while/body/eval_jaxpr/all_gather | solution.py:71
  16.2 0.7 copy-start
  79.3 22.5 %collective-permute-start = (bf16[128,3072]{0,1:T(8,128)(2,1)S(1)}, bf16[128,3072]{0,1:T(8,128)(2,1)S(1)}, u32[]{:S(2)}, u32[]{:S(2)}) collective-permute-start(bf16[128,3072]{0,1:T(8,128)(2,1)S(1)} %get-tuple-element.517), channel_id=1, source_target_pairs={{0,1},{1,2},{2,3},{4,5},{5,6},{6,7},{8,9},{9,10},{10,11},{12,13},{... | collective-permute-start | bytes 2359304 | tf_op jit(solution)/shard_map/while/body/eval_jaxpr/ppermute | solution.py:14
  102.1 156.6 %copy-start.1 = (s32[32]{0:T(128)S(1)}, s32[32]{0:T(128)}, u32[]{:S(2)}) copy-start(s32[32]{0:T(128)} %get-tuple-element.563) | copy-start | bytes 388 | tf_op jit(solution)/shard_map/while
  102.1 156.6 %all-gather.2.cloned.1.call-start = ((), (), s32[]{:S(2)}) async-start(), calls=%async_computation | async-start | bytes 8650752 | tf_op jit(solution)/shard_map/while/body/eval_jaxpr/all_gather | solution.py:71
  104.5 0.7 copy-start
  262.2 21.6 %collective-permute-start = (bf16[128,3072]{0,1:T(8,128)(2,1)S(1)}, bf16[128,3072]{0,1:T(8,128)(2,1)S(1)}, u32[]{:S(2)}, u32[]{:S(2)}) collective-permute-start(bf16[128,3072]{0,1:T(8,128)(2,1)S(1)} %get-tuple-element.517), channel_id=1, source_target_pairs={{0,1},{1,2},{2,3},{4,5},{5,6},{6,7},{8,9},{9,10},{10,11},{12,13},{... | collective-permute-start | bytes 2359304 | tf_op jit(solution)/shard_map/while/body/eval_jaxpr/ppermute | solution.py:14
  284.1 159.5 %copy-start.1 = (s32[32]{0:T(128)S(1)}, s32[32]{0:T(128)}, u32[]{:S(2)}) copy-start(s32[32]{0:T(128)} %get-tuple-element.563) | copy-start | bytes 388 | tf_op jit(solution)/shard_map/while
  284.1 159.5 %all-gather.2.cloned.1.call-start = ((), (), s32[]{:S(2)}) async-start(), calls=%async_computation | async-start | bytes 8650752 | tf_op jit(solution)/shard_map/while/body/eval_jaxpr/all_gather | solution.py:71
  286.5 0.7 copy-start
  447.1 117.8 %collective-permute-start = (bf16[128,3072]{0,1:T(8,128)(2,1)S(1)}, bf16[128,3072]{0,1:T(8,128)(2,1)S(1)}, u32[]{:S(2)}, u32[]{:S(2)}) collective-permute-start(bf16[128,3072]{0,1:T(8,128)(2,1)S(1)} %get-tuple-element.517), channel_id=1, source_target_pairs={{0,1},{1,2},{2,3},{4,5},{5,6},{6,7},{8,9},{9,10},{10,11},{12,13},{... | collective-permute-start | bytes 2359304 | tf_op jit(solution)/shard_map/while/body/eval_jaxpr/ppermute | solution.py:14
  565.2 63.4 %copy-start.1 = (s32[32]{0:T(128)S(1)}, s32[32]{0:T(128)}, u32[]{:S(2)}) copy-start(s32[32]{0:T(128)} %get-tuple-element.563) | copy-start | bytes 388 | tf_op jit(solution)/shard_map/while
  565.2 63.4 %all-gather.2.cloned.1.call-start = ((), (), s32[]{:S(2)}) async-start(), calls=%async_computation | async-start | bytes 8650752 | tf_op jit(solution)/shard_map/while/body/eval_jaxpr/all_gather | solution.py:71
  575.6 0.7 copy-start
  729.0 21.6 %collective-permute-start = (bf16[128,3072]{0,1:T(8,128)(2,1)S(1)}, bf16[128,3072]{0,1:T(8,128)(2,1)S(1)}, u32[]{:S(2)}, u32[]{:S(2)}) collective-permute-start(bf16[128,3072]{0,1:T(8,128)(2,1)S(1)} %get-tuple-element.517), channel_id=1, source_target_pairs={{0,1},{1,2},{2,3},{4,5},{5,6},{6,7},{8,9},{9,10},{10,11},{12,13},{... | collective-permute-start | bytes 2359304 | tf_op jit(solution)/shard_map/while/body/eval_jaxpr/ppermute | solution.py:14
Sparse Core Ops, SparseCore 0:
  17.0 58.7 all-gather.1
  105.4 153.2 all-gather.1
  287.4 156.1 all-gather.1
  576.4 52.1 all-gather.1
where the time goes:
time: 763 us; the launch traced here: 760 us
  waiting for transfers between devices  599 us (79%)
  matrix products  87.8 us (12%)
  local copies, waits for them, and re-layouts  27.5 us (4%)
  other arithmetic  23.3 us (3%)
  between operations  13.6 us (2%)
    all_gather x4, waiting for transfers between devices, attend(): kv_all = lax.all_gather(kv_local, 'stretch', axis=0, tiled=True)  421 us
    ppermute x4, waiting for transfers between devices, passed_along(): return lax.ppermute(block, axis, route)  178 us
    sub x4, matrix products, full_attend(): expons = jnp.where(allowed, jnp.exp(masked - row_top), 0.0)  44.6 us
    dot_general x4, matrix products, full_attend(): jnp.einsum('gts,sd->tgd', weights, head_values(gathered, head_idx), preci...  39.2 us
    another operation x8, local copies, waits for them, and re-layouts  16.8 us
  transfers between devices with their start and end apart: 8, of which 8 were waited for; matrix products, arithmetic and copies ran while one was open for 0% of the time, Pallas kernels for 0%

commit v1 on v0

v1 whole, which is shorter than its diff:
```python
import math

import jax
import jax.numpy as jnp
from jax import lax
from jax.experimental import pallas as pl
from jax.experimental.pallas import tpu as pltpu
from jax.sharding import PartitionSpec as P

HEAD = 128
TOK = 128
GRID = 4
SECTIONS = 4
LAYERS = 4
BLOCKS = 2 * GRID * GRID
D = 3072
SLICE = D // SECTIONS
GROUP = SLICE // HEAD
KVW = SECTIONS * HEAD
PIECE = SLICE // (GRID * GRID)
PROWS = TOK + 16
MESH = pl.DeviceIdType.MESH
QSCALE = math.log2(math.e) / math.sqrt(HEAD)
F32 = jnp.float32
BF16 = jnp.bfloat16


def split_two(row):
    high = row.astype(BF16).astype(F32)
    return high, row - high


def stack_rows(rows, width):
    index = lax.broadcasted_iota(jnp.int32, (16, width), 0)
    out = jnp.zeros((16, width), F32)
    for i, row in enumerate(rows):
        out = jnp.where(index == i, row, out)
    return out


def kernel(levels, lengths, latents, weight, shift_tab, scale_tab, gate_tab, out,
           kvbuf, wbuf, w0buf, ybuf, psend, pbuf, statbuf, mods_own, mods, hbuf, qbuf, maskbuf, mbuf, accbuf, kv0,
           s_kvr, s_kvown, s_kvrelay, s_kvsib, s_wzr, s_wzs, s_wloc, s_w1r, s_w1s, s_w2r, s_w2s, s_w3r, s_w3s,
           s_mods, s_modr, s_sts, s_str, s_ps, s_pr, s_kv0, s_outs, s_outr, s_w0):
    c = lax.axis_index("stretch")
    s = lax.axis_index("section")
    core = lax.rem(c, 2)
    chip = c // 2
    x = chip // GRID
    y = lax.rem(chip, GRID)

    def device(xx, yy, kk):
        return (xx * GRID + yy) * 2 + kk

    def remote(src, dst, send, recv, stretch, section):
        return pltpu.make_async_remote_copy(src_ref=src, dst_ref=dst, send_sem=send, recv_sem=recv,
                                            device_id=(stretch, section), device_id_type=MESH)

    def arrived(ref, sem):
        pltpu.make_async_copy(ref, ref, sem).wait()

    barrier = pltpu.get_barrier_semaphore()
    partners = []
    for d in range(1, 4):
        partners.append((c, lax.rem(s + d, SECTIONS)))
        partners.append((device(lax.rem(x + d, GRID), y, core), s))
        partners.append((device(x, lax.rem(y + d, GRID), core), s))
    partners.append((device(x, y, 1 - core), s))
    for partner in partners:
        pl.semaphore_signal(barrier, inc=1, device_id=partner, device_id_type=MESH)

    @pl.when(s == 0)
    def _():
        for i in range(4):
            rows = pl.ds(i * SLICE, SLICE)
            pltpu.make_async_copy(weight.at[0, rows], w0buf.at[rows], s_w0.at[i]).start()

    wown = lax.max(s - 1, 0)

    def own_weight(half):
        return pltpu.make_async_copy(
            weight.at[0, pl.ds(pl.multiple_of(s * SLICE, SLICE), SLICE), pl.ds(half * KVW, KVW)],
            wbuf.at[wown, half], s_wloc.at[half])

    @pl.when(s > 0)
    def _():
        own_weight(0).start()
        own_weight(1).start()

    level = levels[c]
    mods_own[0:1, :] = 1.0 + scale_tab[0, pl.ds(level, 1), :]
    mods_own[1:2, :] = shift_tab[0, pl.ds(level, 1), :]
    mods_own[2:3, :] = gate_tab[0, pl.ds(level, 1), :]
    mods_own[3:8, :] = jnp.zeros((5, D), F32)
    for t in range(SECTIONS):
        @pl.when(s == t)
        def _(t=t):
            mods[t] = mods_own[:, t * SLICE:(t + 1) * SLICE]

    pl.semaphore_wait(barrier, len(partners))

    def mods_copy(t):
        return remote(mods_own.at[:, pl.ds(t * SLICE, SLICE)], mods.at[s], s_mods.at[t], s_modr.at[s], c, t)

    line = jnp.where(core == 0, y * GRID + x, x * GRID + y)
    line_start = jnp.where(core == 0, y * GRID, x * GRID)
    piece_rows = pl.ds(pl.multiple_of(line * PIECE, PIECE), PIECE)

    def wz_copy(t):
        rows = pl.ds(pl.multiple_of(t * SLICE + line * PIECE, PIECE), PIECE)
        columns = pl.ds(pl.multiple_of(core * KVW, KVW), KVW)
        return remote(weight.at[0, rows, columns], wbuf.at[wown, core, piece_rows], s_wzs.at[t], s_wzr.at[wown], c, t)

    for d in range(1, 4):
        t = lax.rem(s + d, SECTIONS)
        mods_copy(t).start()

        @pl.when(s > 0)
        def _(t=t):
            wz_copy(t).start()

    def along_a(d):
        return device(jnp.where(core == 0, lax.rem(x + d, GRID), x), jnp.where(core == 0, y, lax.rem(y + d, GRID)), core)

    def along_b(d):
        return device(jnp.where(core == 0, x, lax.rem(x + d, GRID)), jnp.where(core == 0, lax.rem(y + d, GRID), y), core)

    place_a = jnp.where(core == 0, x, y)
    place_b = jnp.where(core == 0, y, x)
    line_rows = pl.ds(pl.multiple_of(line_start * PIECE, GRID * PIECE), GRID * PIECE)

    def w1_copy(w, d):
        ref = wbuf.at[w, core, piece_rows]
        return remote(ref, ref, s_w1s.at[w, d - 1], s_w1r.at[w, place_a], along_a(d), s)

    def w2_copy(w, d):
        ref = wbuf.at[w, core, line_rows]
        return remote(ref, ref, s_w2s.at[w, d - 1], s_w2r.at[w, place_b], along_b(d), s)

    def w3_copy(w):
        ref = wbuf.at[w, core]
        return remote(ref, ref, s_w3s.at[w], s_w3r.at[w], device(x, y, 1 - core), s)

    def w_step_a(w):
        @pl.when(s != w + 1)
        def _():
            arrived(wbuf.at[w, core, piece_rows], s_wzr.at[w])
            for d in range(1, 4):
                w1_copy(w, d).start()

    def w_step_b(w):
        @pl.when(s != w + 1)
        def _():
            for d in range(1, 4):
                place = lax.rem(place_a + d, GRID)
                rows = pl.ds(pl.multiple_of((line_start + place) * PIECE, PIECE), PIECE)
                arrived(wbuf.at[w, core, rows], s_w1r.at[w, place])
            for d in range(1, 4):
                w2_copy(w, d).start()

    def w_step_c(w):
        @pl.when(s != w + 1)
        def _():
            for d in range(1, 4):
                place = lax.rem(place_b + d, GRID)
                rows = pl.ds(pl.multiple_of(place * GRID * PIECE, GRID * PIECE), GRID * PIECE)
                arrived(wbuf.at[w, core, rows], s_w2r.at[w, place])
            w3_copy(w).start()

    def w_step_d(w):
        @pl.when(s != w + 1)
        def _():
            arrived(wbuf.at[w, 1 - core], s_w3r.at[w])

        @pl.when(s == w + 1)
        def _():
            own_weight(0).wait()
            own_weight(1).wait()

    my_length = lengths[c]

    def finished(keys, values):
        live = lax.broadcasted_iota(jnp.int32, (TOK, HEAD), 0) < my_length
        keys = jnp.where(live, keys, keys[0:1, :]).astype(BF16)
        values = jnp.where(live, values, 0.0)
        return keys, values.T.astype(BF16)

    def store_queries(unit_rows):
        for g in range(GROUP):
            qbuf[g * TOK:(g + 1) * TOK, :] = unit_rows[:, g * HEAD:(g + 1) * HEAD]

    floats = latents[...].astype(F32)
    row_mean = jnp.mean(floats, axis=-1, keepdims=True)
    row_var = jnp.mean((floats - row_mean) ** 2, axis=-1, keepdims=True)
    row_scale = lax.rsqrt(row_var + 1e-06)

    def kv0_copy(t):
        return remote(kv0.at[t], kvbuf.at[0, c], s_kv0.at[t], s_kvr.at[0, c], c, t)

    @pl.when(s == 0)
    def _():
        total = jnp.zeros((TOK, 2 * KVW), F32)
        for i in range(4):
            columns = slice(i * SLICE, (i + 1) * SLICE)
            part = latents[:, columns].astype(F32)
            normed = ((part - row_mean) * row_scale * mods_own[0:1, columns] + mods_own[1:2, columns]).astype(BF16)
            rows = pl.ds(i * SLICE, SLICE)
            pltpu.make_async_copy(weight.at[0, rows], w0buf.at[rows], s_w0.at[i]).wait()
            total = total + jnp.dot(normed, w0buf[i * SLICE:(i + 1) * SLICE, :], preferred_element_type=F32)
        for t in (2, 1, 3, 0):
            keys, values = finished(total[:, t * HEAD:(t + 1) * HEAD], total[:, KVW + t * HEAD:KVW + (t + 1) * HEAD])
            if t == 0:
                kvbuf[0, c, 0:TOK, :] = keys
                kvbuf[0, c, TOK:2 * TOK, :] = values
            else:
                kv0[t, 0:TOK, :] = keys
                kv0[t, TOK:2 * TOK, :] = values
                kv0_copy(t).start()

    for w in range(LAYERS - 1):
        w_step_a(w)

    @pl.when(s != 0)
    def _():
        arrived(mods.at[0], s_modr.at[0])

    my_columns = pl.ds(pl.multiple_of(s * SLICE, SLICE), SLICE)
    part = latents[:, my_columns].astype(F32)
    store_queries((((part - row_mean) * row_scale * mods[0, 0:1, :] + mods[0, 1:2, :]) * QSCALE).astype(BF16))

    def mask_step(j, carry):
        lane = lax.broadcasted_iota(jnp.int32, (16, 2 * TOK), 1)
        limit = jnp.where(lane < TOK, lengths[2 * j], lengths[2 * j + 1] + TOK)
        maskbuf[j] = jnp.where(lane < limit, 1.0, 0.0).astype(BF16)
        return carry

    lax.fori_loop(0, GRID * GRID, mask_step, 0)
    w_step_b(0)

    @pl.when(s != 0)
    def _():
        arrived(kvbuf.at[0, c], s_kvr.at[0, c])

    def kv_copy(l, block, sem, stretch):
        ref = kvbuf.at[l, block]
        return remote(ref, ref, sem, s_kvr.at[l, block], stretch, s)

    def act(copy, begin):
        if begin:
            copy.start()
        else:
            copy.wait_send()

    def own_copies(l, begin):
        @pl.when(core == 0)
        def _():
            act(kv_copy(l, c, s_kvown.at[l, 6], device(x, y, 1)), begin)

        for d in (2, 1, 3):
            @pl.when(x + d < GRID)
            def _(d=d):
                act(kv_copy(l, c, s_kvown.at[l, d - 1], device(x + d, y, core)), begin)

            @pl.when((y + d < GRID) | ((core == 1) & (x < GRID - 1)))
            def _(d=d):
                act(kv_copy(l, c, s_kvown.at[l, 2 + d], device(x, lax.rem(y + d, GRID), core)), begin)

    def row_relays(l, place, begin):
        block = (x * GRID + place) * 2 + 1
        for d in (2, 1, 3):
            @pl.when(x + d < GRID)
            def _(d=d):
                act(kv_copy(l, block, s_kvrelay.at[l, place, d - 1], device(x + d, y, 1)), begin)

    def relays(l, j, begin):
        xx = j // GRID
        yy = lax.rem(j, GRID)
        act(kv_copy(l, 2 * j + core, s_kvsib.at[l, j], device(x, y, 1 - core)), begin)

        @pl.when((core == 0) & (yy == y))
        def _():
            for d in (2, 1, 3):
                act(kv_copy(l, 2 * j, s_kvrelay.at[l, xx, d - 1], device(x, lax.rem(y + d, GRID), 0)), begin)

        @pl.when((core == 1) & (xx == x))
        def _():
            row_relays(l, yy, begin)

    def late_relays(l, begin):
        @pl.when((core == 1) & (x < GRID - 1))
        def _():
            def body(place, carry):
                if begin:
                    block = (x * GRID + place) * 2 + 1
                    arrived(kvbuf.at[l, block], s_kvr.at[l, block])
                row_relays(l, place, begin)
                return carry

            lax.fori_loop(y + 1, GRID, body, 0)

    def pair(first, second, mask):
        keys = jnp.concatenate([first[0:TOK], second[0:TOK]], axis=0)
        values = jnp.concatenate([jnp.concatenate([first[TOK:], second[TOK:]], axis=1), mask], axis=0)
        score = lax.dot_general(keys, qbuf[...], (((1,), (1,)), ((), ())), preferred_element_type=F32)
        old_top = mbuf[0:1, :]
        top = jnp.maximum(old_top, jnp.max(score, axis=0, keepdims=True))
        probs = jnp.exp2(score - top).astype(BF16)
        mbuf[0:1, :] = top
        accbuf[...] = accbuf[...] * jnp.exp2(old_top - top) + jnp.dot(values, probs, preferred_element_type=F32)

    def out_columns():
        return pl.ds(pl.multiple_of(s * SLICE, SLICE), SLICE)

    def out_remote(l):
        return remote(hbuf.at[l], out.at[0, :, out_columns()], s_outs.at[l], s_outr.at[s], c, l)

    def out_local(l):
        return pltpu.make_async_copy(hbuf.at[l], out.at[0, :, out_columns()], s_outs.at[l])

    def p_copy(w, t):
        return remote(psend.at[w, t], pbuf.at[w, s], s_ps.at[w, t], s_pr.at[w, s], c, t)

    def stat_copy(w, t):
        ref = statbuf.at[w, s]
        return remote(ref, ref, s_sts.at[w, t], s_str.at[w, s], c, t)

    def layer(l, carry):
        own_copies(l, True)
        mbuf[...] = jnp.full(mbuf.shape, -1e30, F32)
        accbuf[...] = jnp.zeros(accbuf.shape, F32)

        def step(j, carry):
            arrived(kvbuf.at[l, 2 * j + core], s_kvr.at[l, 2 * j + core])
            relays(l, j, True)
            arrived(kvbuf.at[l, 2 * j + 1 - core], s_kvr.at[l, 2 * j + 1 - core])
            pair(kvbuf[l, 2 * j], kvbuf[l, 2 * j + 1], maskbuf[j])
            return carry

        lax.fori_loop(0, chip, step, 0)

        @pl.when(l < LAYERS - 1)
        def _():
            w_step_c(l)

        @pl.when(l < LAYERS - 2)
        def _():
            w_step_b(l + 1)

        @pl.when(core == 1)
        def _():
            arrived(kvbuf.at[l, 2 * chip], s_kvr.at[l, 2 * chip])

        first = kvbuf[l, 2 * chip]
        second = kvbuf[l, c]
        lane = lax.broadcasted_iota(jnp.int32, (16, 2 * TOK), 1)
        counted = lane < TOK * (1 + core)
        rows = lax.broadcasted_iota(jnp.int32, (2 * TOK, HEAD), 0)
        second = jnp.where(rows < TOK * (1 + core), second, jnp.zeros_like(second))
        pair(first, second, jnp.where(counted, maskbuf[chip], jnp.zeros((16, 2 * TOK), BF16)))

        inverse = 1.0 / accbuf[TOK:TOK + 1, :]
        for g in range(GROUP):
            columns = slice(g * HEAD, (g + 1) * HEAD)
            attended = (accbuf[0:TOK, g * TOK:(g + 1) * TOK] * inverse[:, g * TOK:(g + 1) * TOK]).T

            @pl.when(l == 0)
            def _(g=g, columns=columns):
                start = pl.ds(pl.multiple_of(s * SLICE + g * HEAD, HEAD), HEAD)
                hbuf[0, :, columns] = latents[:, start]

            @pl.when(l > 0)
            def _(columns=columns):
                hbuf[l, :, columns] = hbuf[lax.max(l - 1, 0), :, columns]

            gate = mods[l, 2:3, columns]
            hbuf[l, :, columns] = (hbuf[l, :, columns].astype(F32) + gate * attended).astype(BF16)

        @pl.when(l < LAYERS - 1)
        def _():
            w = l
            hidden = hbuf[l].astype(F32)
            mean = jnp.mean(hidden, axis=-1, keepdims=True)
            centred = hidden - mean
            square = jnp.sum(centred * centred, axis=-1, keepdims=True)
            lane = lax.broadcasted_iota(jnp.int32, (TOK, HEAD), 1)
            tile = jnp.where(lane == 0, mean, jnp.where(lane == 1, square, 0.0)).T
            statbuf[w, s] = tile[0:8, :]
            for d in (2, 1, 3):
                stat_copy(w, lax.rem(s + d, SECTIONS)).start()

            @pl.when(s != l + 1)
            def _():
                arrived(mods.at[l + 1], s_modr.at[l + 1])

            gain = mods[l + 1, 0:1, :]
            shift = mods[l + 1, 1:2, :]
            ybuf[0:TOK, :] = (centred * gain).astype(BF16)
            ybuf[TOK:PROWS, :] = stack_rows(split_two(gain) + split_two(shift), SLICE).astype(BF16)
            w_step_d(w)
            halves = [jnp.dot(ybuf[...], wbuf[w, i], preferred_element_type=F32) for i in range(2)]
            for i in range(2):
                extra = halves[i][TOK:PROWS]
                extra = stack_rows(split_two(extra[0:1] + extra[1:2]) + split_two(extra[2:3] + extra[3:4]), KVW)
                halves[i] = jnp.concatenate([halves[i][0:TOK], extra], axis=0).astype(BF16)
            for t in range(SECTIONS):
                for i in range(2):
                    psend[w, t, :, i * HEAD:(i + 1) * HEAD] = halves[i][:, t * HEAD:(t + 1) * HEAD]
            for d in (2, 1, 3):
                p_copy(w, lax.rem(s + d, SECTIONS)).start()

        @pl.when(s != l)
        def _():
            out_remote(l).start()

        @pl.when(s == l)
        def _():
            out_local(l).start()

        late_relays(l, True)

        @pl.when(l < LAYERS - 1)
        def _():
            w = l
            for d in range(1, 4):
                t = lax.rem(s + d, SECTIONS)
                arrived(statbuf.at[w, t], s_str.at[w, t])
            stats = jnp.concatenate([statbuf[w, t] for t in range(SECTIONS)] + [jnp.zeros((TOK - 8 * SECTIONS, HEAD), F32)], axis=0).T
            means = [stats[:, 8 * t:8 * t + 1] for t in range(SECTIONS)]
            squares = [stats[:, 8 * t + 1:8 * t + 2] for t in range(SECTIONS)]
            mean = sum(means) / SECTIONS
            offsets = [m - mean for m in means]
            variance = sum(sq + SLICE * o * o for sq, o in zip(squares, offsets)) / D
            scale = lax.rsqrt(variance + 1e-06)
            gain = mods[l + 1, 0:1, :]
            shift = mods[l + 1, 1:2, :]
            store_queries((((hbuf[l].astype(F32) - mean) * scale * gain + shift) * QSCALE).astype(BF16))
            pbuf[w, s] = psend[w, s]
            for d in range(1, 4):
                t = lax.rem(s + d, SECTIONS)
                arrived(pbuf.at[w, t], s_pr.at[w, t])
            total = jnp.zeros((TOK, 2 * HEAD), F32)
            bias = jnp.zeros((1, 2 * HEAD), F32)
            for t in range(SECTIONS):
                extra = pbuf[w, t, TOK:PROWS, :].astype(F32)
                total = total + pbuf[w, t, 0:TOK, :].astype(F32) + offsets[t] * (extra[0:1] + extra[1:2])
                bias = bias + extra[2:3] + extra[3:4]
            total = total * scale + bias
            keys, values = finished(total[:, 0:HEAD], total[:, HEAD:])
            kvbuf[l + 1, c, 0:TOK, :] = keys
            kvbuf[l + 1, c, TOK:2 * TOK, :] = values

        return carry

    lax.fori_loop(0, LAYERS, layer, 0)

    def layer_sent(l, carry):
        own_copies(l, False)

        def step(j, carry):
            relays(l, j, False)
            return carry

        lax.fori_loop(0, chip, step, 0)
        late_relays(l, False)

        @pl.when(s != l)
        def _():
            out_remote(l).wait_send()

        return carry

    lax.fori_loop(0, LAYERS, layer_sent, 0)
    out_local(s).wait()
    for d in range(1, 4):
        t = lax.rem(s + d, SECTIONS)
        mods_copy(t).wait_send()

        @pl.when(s > 0)
        def _(t=t):
            wz_copy(t).wait_send()

    @pl.when(s == 0)
    def _():
        for t in range(1, SECTIONS):
            kv0_copy(t).wait_send()

    def plane_sent(w, carry):
        for d in range(1, 4):
            t = lax.rem(s + d, SECTIONS)
            stat_copy(w, t).wait_send()
            p_copy(w, t).wait_send()

        @pl.when(s != w + 1)
        def _():
            for d in range(1, 4):
                w1_copy(w, d).wait_send()
                w2_copy(w, d).wait_send()
            w3_copy(w).wait_send()

        return carry

    lax.fori_loop(0, LAYERS - 1, plane_sent, 0)
    for d in range(1, 4):
        t = lax.rem(s + d, SECTIONS)
        arrived(out.at[0, :, pl.ds(pl.multiple_of(t * SLICE, SLICE), SLICE)], s_outr.at[t])


def shards(latents, noise_levels, frame_lengths, kv_weight, mod_shift, mod_scale, mod_gate):
    dma = pltpu.SemaphoreType.DMA
    smem = pl.BlockSpec(memory_space=pltpu.SMEM)
    vmem = pl.BlockSpec(memory_space=pltpu.VMEM)
    anywhere = pl.BlockSpec(memory_space=pl.ANY)
    wide = LAYERS - 1
    return pl.pallas_call(
        kernel,
        out_shape=jax.ShapeDtypeStruct((1, TOK, D), BF16),
        in_specs=[smem, smem, vmem, anywhere, vmem, vmem, vmem],
        out_specs=anywhere,
        scratch_shapes=[
            pltpu.VMEM((LAYERS, BLOCKS, 2 * TOK, HEAD), BF16),
            pltpu.VMEM((wide, 2, SLICE, KVW), BF16),
            pltpu.VMEM((D, 2 * KVW), BF16),
            pltpu.VMEM((PROWS, SLICE), BF16),
            pltpu.VMEM((wide, SECTIONS, PROWS, 2 * HEAD), BF16),
            pltpu.VMEM((wide, SECTIONS, PROWS, 2 * HEAD), BF16),
            pltpu.VMEM((wide, SECTIONS, 8, HEAD), F32),
            pltpu.VMEM((8, D), F32),
            pltpu.VMEM((LAYERS, 8, SLICE), F32),
            pltpu.VMEM((LAYERS, TOK, SLICE), BF16),
            pltpu.VMEM((SLICE, HEAD), BF16),
            pltpu.VMEM((GRID * GRID, 16, 2 * TOK), BF16),
            pltpu.VMEM((8, SLICE), F32),
            pltpu.VMEM((PROWS, SLICE), F32),
            pltpu.VMEM((SECTIONS, 2 * TOK, HEAD), BF16),
            dma((LAYERS, BLOCKS)), dma((LAYERS, 7)), dma((LAYERS, GRID, 3)), dma((LAYERS, GRID * GRID)),
            dma((wide,)), dma((SECTIONS,)), dma((2,)), dma((wide, GRID)), dma((wide, 3)), dma((wide, GRID)),
            dma((wide, 3)), dma((wide,)), dma((wide,)),
            dma((SECTIONS,)), dma((SECTIONS,)), dma((wide, SECTIONS)), dma((wide, SECTIONS)),
            dma((wide, SECTIONS)), dma((wide, SECTIONS)), dma((SECTIONS,)), dma((LAYERS,)), dma((SECTIONS,)), dma((4,)),
        ],
        compiler_params=pltpu.CompilerParams(
            collective_id=0, has_side_effects=True, vmem_limit_bytes=56 * 1024 * 1024
        ),
    )(noise_levels, frame_lengths, latents, kv_weight, mod_shift, mod_scale, mod_gate)


def solution(mesh):
    in_specs = (
        P("stretch", None),
        P(),
        P(),
        P("section", None, None),
        P("section", None, None),
        P("section", None, None),
        P("section", None, None),
    )
    out_specs = P("section", "stretch", None)
    return jax.shard_map(shards, mesh=mesh, in_specs=in_specs, out_specs=out_specs, check_vma=False)
```

time: 763 us -> 289 us (0.38)
  the two profiles are of different devices: /device:TPU:96 before, /device:TPU:31 now
where the time goes in v1:
time: 289 us; the launch traced here: 287 us
  Pallas kernels  285 us (99%)
    pallas_call x1, Pallas kernels, shards(): pl.pallas_call(kernel, out_shape=jax.ShapeDtypeStruct((1, TOK, D), BF16),...  285 us

profile of v1, /device:TPU:31, one launch (start us, length us, event | category | flops | bytes accessed | tf_op | source)
XLA Modules:
  0.0 286.8 jit_solution(10083732051165901105)
XLA Ops:
  0.0 284.7 %shard_map.73 = bf16[1,128,3072]{2,1,0:T(8,128)(2,1)} custom-call(s32[32]{0:T(128)} %levels.1, s32[32]{0:T(128)} %lengths.1, bf16[128,3072]{1,0:T(8,128)(2,1)} %latents.1, bf16[1,3072,1024]{2,1,0:T(8,128)(2,1)} %weight.1, f32[1,16,3072]{2,1,0:T(8,128)} %shift_tab.1, f32[1,16,3072]{2,1,0:T(8,128)} %scale_tab.1, f32[1,16,3072]{2,1,0:T(8,128)} %gate_tab.1), custom_call_target="tpu_custom_call" | custom-call | tf_op jit(solution)/shard_map/pallas_call | solution.py:514
  284.7 2.1 copy.9

commit v2 on v1

--- a/solution.py
+++ b/solution.py
@@ -265,38 +265,55 @@
             def _(d=d):
                 act(kv_copy(l, c, s_kvown.at[l, 2 + d], device(x, lax.rem(y + d, GRID), core)), begin)
 
-    def row_relays(l, place, begin):
-        block = (x * GRID + place) * 2 + 1
-        for d in (2, 1, 3):
-            @pl.when(x + d < GRID)
-            def _(d=d):
-                act(kv_copy(l, block, s_kvrelay.at[l, place, d - 1], device(x + d, y, 1)), begin)
-
-    def relays(l, j, begin):
-        xx = j // GRID
-        yy = lax.rem(j, GRID)
-        act(kv_copy(l, 2 * j + core, s_kvsib.at[l, j], device(x, y, 1 - core)), begin)
-
-        @pl.when((core == 0) & (yy == y))
-        def _():
-            for d in (2, 1, 3):
-                act(kv_copy(l, 2 * j, s_kvrelay.at[l, xx, d - 1], device(x, lax.rem(y + d, GRID), 0)), begin)
-
-        @pl.when((core == 1) & (xx == x))
-        def _():
-            row_relays(l, yy, begin)
-
-    def late_relays(l, begin):
-        @pl.when((core == 1) & (x < GRID - 1))
-        def _():
-            def body(place, carry):
+    def sibling_copy(l, j):
+        return kv_copy(l, 2 * j + core, s_kvsib.at[l, j], device(x, y, 1 - core))
+
+    def own_core_arrived(l, j):
+        arrived(kvbuf.at[l, 2 * j + core], s_kvr.at[l, 2 * j + core])
+
+    def column_relays(l, begin):
+        def body(xx, carry):
+            j = xx * GRID + y
+            if begin:
+                own_core_arrived(l, j)
+
+            @pl.when(core == 0)
+            def _():
+                for d in (2, 1, 3):
+                    act(kv_copy(l, 2 * j, s_kvrelay.at[l, xx, d - 1], device(x, lax.rem(y + d, GRID), 0)), begin)
+
+            act(sibling_copy(l, j), begin)
+            return carry
+
+        lax.fori_loop(0, x, body, 0)
+
+    def row_relays(l, begin):
+        for e in (1, 3, 2):
+            place = lax.rem(y + e, GRID)
+            j = x * GRID + place
+
+            @pl.when((place < y) | ((core == 1) & (x < GRID - 1)))
+            def _(j=j, place=place):
                 if begin:
-                    block = (x * GRID + place) * 2 + 1
-                    arrived(kvbuf.at[l, block], s_kvr.at[l, block])
-                row_relays(l, place, begin)
-                return carry
-
-            lax.fori_loop(y + 1, GRID, body, 0)
+                    own_core_arrived(l, j)
+
+                @pl.when((core == 1) & (x < GRID - 1))
+                def _():
+                    for d in (2, 1, 3):
+                        @pl.when(x + d < GRID)
+                        def _(d=d):
+                            act(kv_copy(l, 2 * j + 1, s_kvrelay.at[l, place, d - 1], device(x + d, y, 1)), begin)
+
+                @pl.when(place < y)
+                def _():
+                    act(sibling_copy(l, j), begin)
+
+    def other_relays(l, xx, begin):
+        for e in (1, 3, 2):
+            j = xx * GRID + lax.rem(y + e, GRID)
+            if begin:
+                own_core_arrived(l, j)
+            act(sibling_copy(l, j), begin)
 
     def pair(first, second, mask):
         keys = jnp.concatenate([first[0:TOK], second[0:TOK]], axis=0)
@@ -330,13 +347,27 @@
         accbuf[...] = jnp.zeros(accbuf.shape, F32)
 
         def step(j, carry):
-            arrived(kvbuf.at[l, 2 * j + core], s_kvr.at[l, 2 * j + core])
-            relays(l, j, True)
             arrived(kvbuf.at[l, 2 * j + 1 - core], s_kvr.at[l, 2 * j + 1 - core])
             pair(kvbuf[l, 2 * j], kvbuf[l, 2 * j + 1], maskbuf[j])
             return carry
 
-        lax.fori_loop(0, chip, step, 0)
+        column_relays(l, True)
+
+        @pl.when((l == 0) | (x == 0))
+        def _():
+            row_relays(l, True)
+
+        def row(xx, carry):
+            other_relays(l, xx, True)
+            lax.fori_loop(xx * GRID, (xx + 1) * GRID, step, 0)
+
+            @pl.when((l > 0) & (xx == 0))
+            def _():
+                row_relays(l, True)
+
+            return carry
+
+        lax.fori_loop(0, x, row, 0)
 
         @pl.when(l < LAYERS - 1)
         def _():
@@ -345,6 +376,8 @@
         @pl.when(l < LAYERS - 2)
         def _():
             w_step_b(l + 1)
+
+        lax.fori_loop(x * GRID, chip, step, 0)
 
         @pl.when(core == 1)
         def _():
@@ -416,8 +449,6 @@
         def _():
             out_local(l).start()
 
-        late_relays(l, True)
-
         @pl.when(l < LAYERS - 1)
         def _():
             w = l
@@ -456,12 +487,14 @@
     def layer_sent(l, carry):
         own_copies(l, False)
 
-        def step(j, carry):
-            relays(l, j, False)
+        column_relays(l, False)
+        row_relays(l, False)
+
+        def row(xx, carry):
+            other_relays(l, xx, False)
             return carry
 
-        lax.fori_loop(0, chip, step, 0)
-        late_relays(l, False)
+        lax.fori_loop(0, x, row, 0)
 
         @pl.when(s != l)
         def _():

time: 289 us -> 130 us (0.45)
  Pallas kernels: 285 us -> 128 us
    pallas_call x1, Pallas kernels: 285 us -> 128 us  [shards(): pl.pallas_call(kernel, out_shape=jax.ShapeDtypeStruct((1, TOK, D), BF16),...]
where the time goes in v2:
time: 130 us
  Pallas kernels  128 us (98%)
  local copies, waits for them, and re-layouts  2.06 us (2%)
    pallas_call x1, Pallas kernels, shards(): pl.pallas_call(kernel, out_shape=jax.ShapeDtypeStruct((1, TOK, D), BF16),...  128 us

profile of v2, /device:TPU:31, one launch (start us, length us, event | category | flops | bytes accessed | tf_op | source)
XLA Modules:
  0.0 129.8 jit_solution(16335037809060383766)
XLA Ops:
  0.0 127.7 %shard_map.73 = bf16[1,128,3072]{2,1,0:T(8,128)(2,1)} custom-call(s32[32]{0:T(128)} %levels.1, s32[32]{0:T(128)} %lengths.1, bf16[128,3072]{1,0:T(8,128)(2,1)} %latents.1, bf16[1,3072,1024]{2,1,0:T(8,128)(2,1)} %weight.1, f32[1,16,3072]{2,1,0:T(8,128)} %shift_tab.1, f32[1,16,3072]{2,1,0:T(8,128)} %scale_tab.1, f32[1,16,3072]{2,1,0:T(8,128)} %gate_tab.1), custom_call_target="tpu_custom_call" | custom-call | tf_op jit(solution)/shard_map/pallas_call | solution.py:547
  127.7 2.1 %copy.9 = bf16[1,128,3072]{2,1,0:T(8,128)(2,1)} copy(bf16[1,128,3072]{2,1,0:T(8,128)(2,1)} %shard_map.73) | data formatting | bytes 1572864

commit v3 on v2

--- a/solution.py
+++ b/solution.py
@@ -39,7 +39,7 @@
 
 
 def kernel(levels, lengths, latents, weight, shift_tab, scale_tab, gate_tab, out,
-           kvbuf, wbuf, w0buf, ybuf, psend, pbuf, statbuf, mods_own, mods, hbuf, qbuf, maskbuf, mbuf, accbuf, kv0,
+           kvbuf, wbuf, w0buf, ybuf, psend, pbuf, statbuf, mods_own, mods, hbuf, qbuf, maskbuf, mbuf, accbuf, sbuf, kv0,
            s_kvr, s_kvown, s_kvrelay, s_kvsib, s_wzr, s_wzs, s_wloc, s_w1r, s_w1s, s_w2r, s_w2s, s_w3r, s_w3s,
            s_mods, s_modr, s_sts, s_str, s_ps, s_pr, s_kv0, s_outs, s_outr, s_w0):
     c = lax.axis_index("stretch")
@@ -97,8 +97,6 @@
         def _(t=t):
             mods[t] = mods_own[:, t * SLICE:(t + 1) * SLICE]
 
-    pl.semaphore_wait(barrier, len(partners))
-
     def mods_copy(t):
         return remote(mods_own.at[:, pl.ds(t * SLICE, SLICE)], mods.at[s], s_mods.at[t], s_modr.at[s], c, t)
 
@@ -110,14 +108,6 @@
         rows = pl.ds(pl.multiple_of(t * SLICE + line * PIECE, PIECE), PIECE)
         columns = pl.ds(pl.multiple_of(core * KVW, KVW), KVW)
         return remote(weight.at[0, rows, columns], wbuf.at[wown, core, piece_rows], s_wzs.at[t], s_wzr.at[wown], c, t)
-
-    for d in range(1, 4):
-        t = lax.rem(s + d, SECTIONS)
-        mods_copy(t).start()
-
-        @pl.when(s > 0)
-        def _(t=t):
-            wz_copy(t).start()
 
     def along_a(d):
         return device(jnp.where(core == 0, lax.rem(x + d, GRID), x), jnp.where(core == 0, y, lax.rem(y + d, GRID)), core)
@@ -189,13 +179,24 @@
         for g in range(GROUP):
             qbuf[g * TOK:(g + 1) * TOK, :] = unit_rows[:, g * HEAD:(g + 1) * HEAD]
 
+    def kv0_copy(t):
+        return remote(kv0.at[t], kvbuf.at[0, c], s_kv0.at[t], s_kvr.at[0, c], c, t)
+
+    def greet():
+        pl.semaphore_wait(barrier, len(partners))
+        for d in range(1, 4):
+            t = lax.rem(s + d, SECTIONS)
+            mods_copy(t).start()
+
+            @pl.when(s > 0)
+            def _(t=t):
+                wz_copy(t).start()
+
+    pl.when(s > 0)(greet)
     floats = latents[...].astype(F32)
     row_mean = jnp.mean(floats, axis=-1, keepdims=True)
     row_var = jnp.mean((floats - row_mean) ** 2, axis=-1, keepdims=True)
     row_scale = lax.rsqrt(row_var + 1e-06)
-
-    def kv0_copy(t):
-        return remote(kv0.at[t], kvbuf.at[0, c], s_kv0.at[t], s_kvr.at[0, c], c, t)
 
     @pl.when(s == 0)
     def _():
@@ -207,6 +208,7 @@
             rows = pl.ds(i * SLICE, SLICE)
             pltpu.make_async_copy(weight.at[0, rows], w0buf.at[rows], s_w0.at[i]).wait()
             total = total + jnp.dot(normed, w0buf[i * SLICE:(i + 1) * SLICE, :], preferred_element_type=F32)
+        greet()
         for t in (2, 1, 3, 0):
             keys, values = finished(total[:, t * HEAD:(t + 1) * HEAD], total[:, KVW + t * HEAD:KVW + (t + 1) * HEAD])
             if t == 0:
@@ -287,13 +289,12 @@
 
         lax.fori_loop(0, x, body, 0)
 
-    def row_relays(l, begin):
+    def row_relays(l, begin, earlier, later):
         for e in (1, 3, 2):
             place = lax.rem(y + e, GRID)
             j = x * GRID + place
 
-            @pl.when((place < y) | ((core == 1) & (x < GRID - 1)))
-            def _(j=j, place=place):
+            def hand_on(j=j, place=place):
                 if begin:
                     own_core_arrived(l, j)
 
@@ -308,6 +309,11 @@
                 def _():
                     act(sibling_copy(l, j), begin)
 
+            if earlier:
+                pl.when(place < y)(hand_on)
+            if later:
+                pl.when((place > y) & (core == 1) & (x < GRID - 1))(hand_on)
+
     def other_relays(l, xx, begin):
         for e in (1, 3, 2):
             j = xx * GRID + lax.rem(y + e, GRID)
@@ -315,15 +321,42 @@
                 own_core_arrived(l, j)
             act(sibling_copy(l, j), begin)
 
-    def pair(first, second, mask):
-        keys = jnp.concatenate([first[0:TOK], second[0:TOK]], axis=0)
-        values = jnp.concatenate([jnp.concatenate([first[TOK:], second[TOK:]], axis=1), mask], axis=0)
+    def row_blocks(l, xx, last):
+        blocks = []
+        for yy in range(GRID):
+            first = (xx * GRID + (jnp.minimum(yy, y) if last else yy)) * 2
+            second = first + 1
+            if last:
+                second = jnp.where(yy < y, second, first + core)
+            blocks += [(first, yy <= y), (second, (yy < y) | ((yy == y) & (core == 1)))]
+        return blocks
+
+    def scores(l, xx, slot, last):
+        keys = jnp.concatenate([kvbuf[l, block, 0:TOK] for block, _ in row_blocks(l, xx, last)], axis=0)
         score = lax.dot_general(keys, qbuf[...], (((1,), (1,)), ((), ())), preferred_element_type=F32)
+        sbuf[slot] = score
+        return jnp.max(score, axis=0, keepdims=True)
+
+    def mix(l, xx, slot, last):
         old_top = mbuf[0:1, :]
-        top = jnp.maximum(old_top, jnp.max(score, axis=0, keepdims=True))
-        probs = jnp.exp2(score - top).astype(BF16)
+        top = mbuf[1:2, :]
+        blocks = row_blocks(l, xx, last)
+        values = jnp.concatenate([kvbuf[l, block, TOK:] for block, _ in blocks], axis=1)
+        masks = jnp.concatenate([maskbuf[xx * GRID + yy] for yy in range(GRID)], axis=1)
+        if last:
+            lane = lax.broadcasted_iota(jnp.int32, (TOK + 16, 2 * GRID * TOK), 1)
+            counted = lane < TOK * (2 * y + 1 + core)
+            both = jnp.concatenate([values, masks], axis=0)
+            both = jnp.where(counted, both, jnp.zeros_like(both))
+        else:
+            both = jnp.concatenate([values, masks], axis=0)
+        probs = jnp.exp2(sbuf[slot] - top).astype(BF16)
+        accbuf[...] = accbuf[...] * jnp.exp2(old_top - top) + jnp.dot(both, probs, preferred_element_type=F32)
+
+    def next_top(found):
+        top = mbuf[1:2, :]
         mbuf[0:1, :] = top
-        accbuf[...] = accbuf[...] * jnp.exp2(old_top - top) + jnp.dot(values, probs, preferred_element_type=F32)
+        mbuf[1:2, :] = jnp.maximum(top, found)
 
     def out_columns():
         return pl.ds(pl.multiple_of(s * SLICE, SLICE), SLICE)
@@ -346,28 +379,64 @@
         mbuf[...] = jnp.full(mbuf.shape, -1e30, F32)
         accbuf[...] = jnp.zeros(accbuf.shape, F32)
 
-        def step(j, carry):
+        def other_core_arrived(j):
             arrived(kvbuf.at[l, 2 * j + 1 - core], s_kvr.at[l, 2 * j + 1 - core])
-            pair(kvbuf[l, 2 * j], kvbuf[l, 2 * j + 1], maskbuf[j])
-            return carry
+
+        def row_arrived(xx):
+            for yy in range(GRID):
+                other_core_arrived(xx * GRID + yy)
+
+        def own_row_relays():
+            @pl.when(l > 0)
+            def _():
+                row_relays(l, True, True, True)
+
+        def own_row_arrived():
+            lax.fori_loop(x * GRID, chip, lambda j, carry: (other_core_arrived(j), carry)[1], 0)
+
+            @pl.when(core == 1)
+            def _():
+                arrived(kvbuf.at[l, 2 * chip], s_kvr.at[l, 2 * chip])
 
         column_relays(l, True)
 
-        @pl.when((l == 0) | (x == 0))
-        def _():
-            row_relays(l, True)
-
-        def row(xx, carry):
-            other_relays(l, xx, True)
-            lax.fori_loop(xx * GRID, (xx + 1) * GRID, step, 0)
-
-            @pl.when((l > 0) & (xx == 0))
-            def _():
-                row_relays(l, True)
-
-            return carry
-
-        lax.fori_loop(0, x, row, 0)
+        @pl.when(l == 0)
+        def _():
+            row_relays(l, True, True, True)
+
+        for ahead in range(2):
+            @pl.when(x > ahead)
+            def _(ahead=ahead):
+                other_relays(l, ahead, True)
+
+        pl.when(x < 2)(own_row_relays)
+
+        for slot in range(2):
+            @pl.when((x > 0) & (lax.rem(x, 2) == 1 - slot))
+            def _(slot=slot):
+                row_arrived(0)
+                next_top(scores(l, 0, slot, False))
+
+        @pl.when(x == 0)
+        def _():
+            own_row_arrived()
+            next_top(scores(l, 0, 1, True))
+
+        for t in range(GRID - 1):
+            @pl.when(x + t >= GRID - 1)
+            def _(t=t):
+                row = x + t - (GRID - 1)
+                if t == 0:
+                    other_relays(l, row + 2, True)
+                if t == 1:
+                    own_row_relays()
+                if t < 2:
+                    row_arrived(row + 1)
+                else:
+                    own_row_arrived()
+                found = scores(l, row + 1, (t + 1) % 2, t == GRID - 2)
+                mix(l, row, t % 2, False)
+                next_top(found)
 
         @pl.when(l < LAYERS - 1)
         def _():
@@ -377,19 +446,7 @@
         def _():
             w_step_b(l + 1)
 
-        lax.fori_loop(x * GRID, chip, step, 0)
-
-        @pl.when(core == 1)
-        def _():
-            arrived(kvbuf.at[l, 2 * chip], s_kvr.at[l, 2 * chip])
-
-        first = kvbuf[l, 2 * chip]
-        second = kvbuf[l, c]
-        lane = lax.broadcasted_iota(jnp.int32, (16, 2 * TOK), 1)
-        counted = lane < TOK * (1 + core)
-        rows = lax.broadcasted_iota(jnp.int32, (2 * TOK, HEAD), 0)
-        second = jnp.where(rows < TOK * (1 + core), second, jnp.zeros_like(second))
-        pair(first, second, jnp.where(counted, maskbuf[chip], jnp.zeros((16, 2 * TOK), BF16)))
+        mix(l, x, 1, True)
 
         inverse = 1.0 / accbuf[TOK:TOK + 1, :]
         for g in range(GROUP):
@@ -440,14 +497,6 @@
                     psend[w, t, :, i * HEAD:(i + 1) * HEAD] = halves[i][:, t * HEAD:(t + 1) * HEAD]
             for d in (2, 1, 3):
                 p_copy(w, lax.rem(s + d, SECTIONS)).start()
-
-        @pl.when(s != l)
-        def _():
-            out_remote(l).start()
-
-        @pl.when(s == l)
-        def _():
-            out_local(l).start()
 
         @pl.when(l < LAYERS - 1)
         def _():
@@ -480,6 +529,14 @@
             kvbuf[l + 1, c, 0:TOK, :] = keys
             kvbuf[l + 1, c, TOK:2 * TOK, :] = values
 
+        @pl.when(s != l)
+        def _():
+            out_remote(l).start()
+
+        @pl.when(s == l)
+        def _():
+            out_local(l).start()
+
         return carry
 
     lax.fori_loop(0, LAYERS, layer, 0)
@@ -488,7 +545,7 @@
         own_copies(l, False)
 
         column_relays(l, False)
-        row_relays(l, False)
+        row_relays(l, False, True, True)
 
         def row(xx, carry):
             other_relays(l, xx, False)
@@ -564,6 +621,7 @@
             pltpu.VMEM((GRID * GRID, 16, 2 * TOK), BF16),
             pltpu.VMEM((8, SLICE), F32),
             pltpu.VMEM((PROWS, SLICE), F32),
+            pltpu.VMEM((2, 2 * GRID * TOK, SLICE), F32),
             pltpu.VMEM((SECTIONS, 2 * TOK, HEAD), BF16),
             dma((LAYERS, BLOCKS)), dma((LAYERS, 7)), dma((LAYERS, GRID, 3)), dma((LAYERS, GRID * GRID)),
             dma((wide,)), dma((SECTIONS,)), dma((2,)), dma((wide, GRID)), dma((wide, 3)), dma((wide, GRID)),

time: 130 us -> 113 us (0.87)
  Pallas kernels: 128 us -> 110 us
    pallas_call x1, Pallas kernels: 128 us -> 110 us  [shards(): pl.pallas_call(kernel, out_shape=jax.ShapeDtypeStruct((1, TOK, D), BF16),...]
where the time goes in v3:
time: 113 us; the launch traced here: 112 us
  Pallas kernels  110 us (97%)
  local copies, waits for them, and re-layouts  2.06 us (2%)
    pallas_call x1, Pallas kernels, shards(): pl.pallas_call(kernel, out_shape=jax.ShapeDtypeStruct((1, TOK, D), BF16),...  110 us

profile of v3, /device:TPU:31, one launch (start us, length us, event | category | flops | bytes accessed | tf_op | source)
XLA Modules:
  0.0 112.4 jit_solution(5819442403426782199)
XLA Ops:
  0.0 110.3 %shard_map.73 = bf16[1,128,3072]{2,1,0:T(8,128)(2,1)} custom-call(s32[32]{0:T(128)} %levels.1, s32[32]{0:T(128)} %lengths.1, bf16[128,3072]{1,0:T(8,128)(2,1)} %latents.1, bf16[1,3072,1024]{2,1,0:T(8,128)(2,1)} %weight.1, f32[1,16,3072]{2,1,0:T(8,128)} %shift_tab.1, f32[1,16,3072]{2,1,0:T(8,128)} %scale_tab.1, f32[1,16,3072]{2,1,0:T(8,128)} %gate_tab.1), custom_call_target="tpu_custom_call" | custom-call | tf_op jit(solution)/shard_map/pallas_call | solution.py:604
  110.3 2.1 %copy.9 = bf16[1,128,3072]{2,1,0:T(8,128)(2,1)} copy(bf16[1,128,3072]{2,1,0:T(8,128)(2,1)} %shard_map.73) | data formatting | bytes 1572864

commit v4 on v3

--- a/solution.py
+++ b/solution.py
@@ -38,10 +38,10 @@
     return out
 
 
-def kernel(levels, lengths, latents, weight, shift_tab, scale_tab, gate_tab, out,
-           kvbuf, wbuf, w0buf, ybuf, psend, pbuf, statbuf, mods_own, mods, hbuf, qbuf, maskbuf, mbuf, accbuf, sbuf, kv0,
-           s_kvr, s_kvown, s_kvrelay, s_kvsib, s_wzr, s_wzs, s_wloc, s_w1r, s_w1s, s_w2r, s_w2s, s_w3r, s_w3s,
-           s_mods, s_modr, s_sts, s_str, s_ps, s_pr, s_kv0, s_outs, s_outr, s_w0):
+def kernel(levels, lengths, latents_in, weight, shift_in, scale_in, gate_in, out,
+           latents, tables, kvbuf, wbuf, w0buf, ybuf, psend, pbuf, statbuf, mods_own, mods, hbuf, qbuf, maskbuf, mbuf, accbuf, sbuf, kv0,
+           s_kvr, s_kvown, s_kvsib, s_wzr, s_wzs, s_wloc, s_w1r, s_w1s, s_w2r, s_w2s, s_w3r, s_w3s,
+           s_mods, s_modr, s_sts, s_str, s_ps, s_pr, s_kv0, s_outs, s_outr, s_w0, s_in):
     c = lax.axis_index("stretch")
     s = lax.axis_index("section")
     core = lax.rem(c, 2)
@@ -59,15 +59,24 @@
     def arrived(ref, sem):
         pltpu.make_async_copy(ref, ref, sem).wait()
 
+    inputs = [pltpu.make_async_copy(shift_in.at[0], tables.at[0], s_in.at[0]),
+              pltpu.make_async_copy(scale_in.at[0], tables.at[1], s_in.at[1]),
+              pltpu.make_async_copy(gate_in.at[0], tables.at[2], s_in.at[2]),
+              pltpu.make_async_copy(latents_in, latents, s_in.at[3])]
+    for copy in inputs:
+        copy.start()
+
     barrier = pltpu.get_barrier_semaphore()
-    partners = []
-    for d in range(1, 4):
-        partners.append((c, lax.rem(s + d, SECTIONS)))
-        partners.append((device(lax.rem(x + d, GRID), y, core), s))
-        partners.append((device(x, lax.rem(y + d, GRID), core), s))
-    partners.append((device(x, y, 1 - core), s))
-    for partner in partners:
-        pl.semaphore_signal(barrier, inc=1, device_id=partner, device_id_type=MESH)
+    for d in range(1, SECTIONS):
+        pl.semaphore_signal(barrier, inc=1, device_id=(c, lax.rem(s + d, SECTIONS)), device_id_type=MESH)
+    pl.semaphore_signal(barrier, inc=1, device_id=(device(x, y, 1 - core), s), device_id_type=MESH)
+
+    def greet_chip(d, carry):
+        other = lax.rem(chip + d, GRID * GRID)
+        pl.semaphore_signal(barrier, inc=1, device_id=(2 * other + core, s), device_id_type=MESH)
+        return carry
+
+    lax.fori_loop(1, GRID * GRID, greet_chip, 0)
 
     @pl.when(s == 0)
     def _():
@@ -88,9 +97,11 @@
         own_weight(1).start()
 
     level = levels[c]
-    mods_own[0:1, :] = 1.0 + scale_tab[0, pl.ds(level, 1), :]
-    mods_own[1:2, :] = shift_tab[0, pl.ds(level, 1), :]
-    mods_own[2:3, :] = gate_tab[0, pl.ds(level, 1), :]
+    for copy in inputs[:3]:
+        copy.wait()
+    mods_own[0:1, :] = 1.0 + tables[1, pl.ds(level, 1), :]
+    mods_own[1:2, :] = tables[0, pl.ds(level, 1), :]
+    mods_own[2:3, :] = tables[2, pl.ds(level, 1), :]
     mods_own[3:8, :] = jnp.zeros((5, D), F32)
     for t in range(SECTIONS):
         @pl.when(s == t)
@@ -183,7 +194,7 @@
         return remote(kv0.at[t], kvbuf.at[0, c], s_kv0.at[t], s_kvr.at[0, c], c, t)
 
     def greet():
-        pl.semaphore_wait(barrier, len(partners))
+        pl.semaphore_wait(barrier, SECTIONS + GRID * GRID - 1)
         for d in range(1, 4):
             t = lax.rem(s + d, SECTIONS)
             mods_copy(t).start()
@@ -193,6 +204,7 @@
                 wz_copy(t).start()
 
     pl.when(s > 0)(greet)
+    inputs[3].wait()
     floats = latents[...].astype(F32)
     row_mean = jnp.mean(floats, axis=-1, keepdims=True)
     row_var = jnp.mean((floats - row_mean) ** 2, axis=-1, keepdims=True)
@@ -227,7 +239,8 @@
         arrived(mods.at[0], s_modr.at[0])
 
     my_columns = pl.ds(pl.multiple_of(s * SLICE, SLICE), SLICE)
-    part = latents[:, my_columns].astype(F32)
+    hbuf[0] = latents[:, my_columns]
+    part = hbuf[0].astype(F32)
     store_queries((((part - row_mean) * row_scale * mods[0, 0:1, :] + mods[0, 1:2, :]) * QSCALE).astype(BF16))
 
     def mask_step(j, carry):
@@ -237,10 +250,10 @@
         return carry
 
     lax.fori_loop(0, GRID * GRID, mask_step, 0)
-    w_step_b(0)
 
     @pl.when(s != 0)
     def _():
+        w_step_b(0)
         arrived(kvbuf.at[0, c], s_kvr.at[0, c])
 
     def kv_copy(l, block, sem, stretch):
@@ -256,70 +269,23 @@
     def own_copies(l, begin):
         @pl.when(core == 0)
         def _():
-            act(kv_copy(l, c, s_kvown.at[l, 6], device(x, y, 1)), begin)
-
-        for d in (2, 1, 3):
-            @pl.when(x + d < GRID)
-            def _(d=d):
-                act(kv_copy(l, c, s_kvown.at[l, d - 1], device(x + d, y, core)), begin)
-
-            @pl.when((y + d < GRID) | ((core == 1) & (x < GRID - 1)))
-            def _(d=d):
-                act(kv_copy(l, c, s_kvown.at[l, 2 + d], device(x, lax.rem(y + d, GRID), core)), begin)
-
-    def sibling_copy(l, j):
-        return kv_copy(l, 2 * j + core, s_kvsib.at[l, j], device(x, y, 1 - core))
-
-    def own_core_arrived(l, j):
-        arrived(kvbuf.at[l, 2 * j + core], s_kvr.at[l, 2 * j + core])
-
-    def column_relays(l, begin):
-        def body(xx, carry):
-            j = xx * GRID + y
+            act(kv_copy(l, c, s_kvown.at[l, chip], device(x, y, 1)), begin)
+
+        def body(other, carry):
+            act(kv_copy(l, c, s_kvown.at[l, other], 2 * other + core), begin)
+            return carry
+
+        lax.fori_loop(chip + 1, GRID * GRID, body, 0)
+
+    def hand_over(l, start, stop, begin):
+        def body(j, carry):
+            block = 2 * j + core
             if begin:
-                own_core_arrived(l, j)
-
-            @pl.when(core == 0)
-            def _():
-                for d in (2, 1, 3):
-                    act(kv_copy(l, 2 * j, s_kvrelay.at[l, xx, d - 1], device(x, lax.rem(y + d, GRID), 0)), begin)
-
-            act(sibling_copy(l, j), begin)
+                arrived(kvbuf.at[l, block], s_kvr.at[l, block])
+            act(kv_copy(l, block, s_kvsib.at[l, j], device(x, y, 1 - core)), begin)
             return carry
 
-        lax.fori_loop(0, x, body, 0)
-
-    def row_relays(l, begin, earlier, later):
-        for e in (1, 3, 2):
-            place = lax.rem(y + e, GRID)
-            j = x * GRID + place
-
-            def hand_on(j=j, place=place):
-                if begin:
-                    own_core_arrived(l, j)
-
-                @pl.when((core == 1) & (x < GRID - 1))
-                def _():
-                    for d in (2, 1, 3):
-                        @pl.when(x + d < GRID)
-                        def _(d=d):
-                            act(kv_copy(l, 2 * j + 1, s_kvrelay.at[l, place, d - 1], device(x + d, y, 1)), begin)
-
-                @pl.when(place < y)
-                def _():
-                    act(sibling_copy(l, j), begin)
-
-            if earlier:
-                pl.when(place < y)(hand_on)
-            if later:
-                pl.when((place > y) & (core == 1) & (x < GRID - 1))(hand_on)
-
-    def other_relays(l, xx, begin):
-        for e in (1, 3, 2):
-            j = xx * GRID + lax.rem(y + e, GRID)
-            if begin:
-                own_core_arrived(l, j)
-            act(sibling_copy(l, j), begin)
+        lax.fori_loop(start, stop, body, 0)
 
     def row_blocks(l, xx, last):
         blocks = []
@@ -362,10 +328,10 @@
         return pl.ds(pl.multiple_of(s * SLICE, SLICE), SLICE)
 
     def out_remote(l):
-        return remote(hbuf.at[l], out.at[0, :, out_columns()], s_outs.at[l], s_outr.at[s], c, l)
+        return remote(hbuf.at[l + 1], out.at[0, :, out_columns()], s_outs.at[l], s_outr.at[s], c, l)
 
     def out_local(l):
-        return pltpu.make_async_copy(hbuf.at[l], out.at[0, :, out_columns()], s_outs.at[l])
+        return pltpu.make_async_copy(hbuf.at[l + 1], out.at[0, :, out_columns()], s_outs.at[l])
 
     def p_copy(w, t):
         return remote(psend.at[w, t], pbuf.at[w, s], s_ps.at[w, t], s_pr.at[w, s], c, t)
@@ -376,6 +342,11 @@
 
     def layer(l, carry):
         own_copies(l, True)
+
+        @pl.when((l == 0) & (s == 0))
+        def _():
+            w_step_b(0)
+
         mbuf[...] = jnp.full(mbuf.shape, -1e30, F32)
         accbuf[...] = jnp.zeros(accbuf.shape, F32)
 
@@ -386,11 +357,6 @@
             for yy in range(GRID):
                 other_core_arrived(xx * GRID + yy)
 
-        def own_row_relays():
-            @pl.when(l > 0)
-            def _():
-                row_relays(l, True, True, True)
-
         def own_row_arrived():
             lax.fori_loop(x * GRID, chip, lambda j, carry: (other_core_arrived(j), carry)[1], 0)
 
@@ -398,18 +364,7 @@
             def _():
                 arrived(kvbuf.at[l, 2 * chip], s_kvr.at[l, 2 * chip])
 
-        column_relays(l, True)
-
-        @pl.when(l == 0)
-        def _():
-            row_relays(l, True, True, True)
-
-        for ahead in range(2):
-            @pl.when(x > ahead)
-            def _(ahead=ahead):
-                other_relays(l, ahead, True)
-
-        pl.when(x < 2)(own_row_relays)
+        hand_over(l, 0, jnp.minimum(chip, 2 * GRID), True)
 
         for slot in range(2):
             @pl.when((x > 0) & (lax.rem(x, 2) == 1 - slot))
@@ -426,19 +381,18 @@
             @pl.when(x + t >= GRID - 1)
             def _(t=t):
                 row = x + t - (GRID - 1)
-                if t == 0:
-                    other_relays(l, row + 2, True)
-                if t == 1:
-                    own_row_relays()
+                if t < 2:
+                    hand_over(l, (row + 2) * GRID, jnp.minimum((row + 3) * GRID, chip), True)
                 if t < 2:
                     row_arrived(row + 1)
                 else:
+                    pl.when(l < LAYERS - 1)(lambda: w_step_c(l))
                     own_row_arrived()
                 found = scores(l, row + 1, (t + 1) % 2, t == GRID - 2)
                 mix(l, row, t % 2, False)
                 next_top(found)
 
-        @pl.when(l < LAYERS - 1)
+        @pl.when((l < LAYERS - 1) & (x == 0))
         def _():
             w_step_c(l)
 
@@ -453,22 +407,13 @@
             columns = slice(g * HEAD, (g + 1) * HEAD)
             attended = (accbuf[0:TOK, g * TOK:(g + 1) * TOK] * inverse[:, g * TOK:(g + 1) * TOK]).T
 
-            @pl.when(l == 0)
-            def _(g=g, columns=columns):
-                start = pl.ds(pl.multiple_of(s * SLICE + g * HEAD, HEAD), HEAD)
-                hbuf[0, :, columns] = latents[:, start]
-
-            @pl.when(l > 0)
-            def _(columns=columns):
-                hbuf[l, :, columns] = hbuf[lax.max(l - 1, 0), :, columns]
-
             gate = mods[l, 2:3, columns]
-            hbuf[l, :, columns] = (hbuf[l, :, columns].astype(F32) + gate * attended).astype(BF16)
+            hbuf[l + 1, :, columns] = (hbuf[l, :, columns].astype(F32) + gate * attended).astype(BF16)
 
         @pl.when(l < LAYERS - 1)
         def _():
             w = l
-            hidden = hbuf[l].astype(F32)
+            hidden = hbuf[l + 1].astype(F32)
             mean = jnp.mean(hidden, axis=-1, keepdims=True)
             centred = hidden - mean
             square = jnp.sum(centred * centred, axis=-1, keepdims=True)
@@ -513,7 +458,7 @@
             scale = lax.rsqrt(variance + 1e-06)
             gain = mods[l + 1, 0:1, :]
             shift = mods[l + 1, 1:2, :]
-            store_queries((((hbuf[l].astype(F32) - mean) * scale * gain + shift) * QSCALE).astype(BF16))
+            store_queries((((hbuf[l + 1].astype(F32) - mean) * scale * gain + shift) * QSCALE).astype(BF16))
             pbuf[w, s] = psend[w, s]
             for d in range(1, 4):
                 t = lax.rem(s + d, SECTIONS)
@@ -544,14 +489,7 @@
     def layer_sent(l, carry):
         own_copies(l, False)
 
-        column_relays(l, False)
-        row_relays(l, False, True, True)
-
-        def row(xx, carry):
-            other_relays(l, xx, False)
-            return carry
-
-        lax.fori_loop(0, x, row, 0)
+        hand_over(l, 0, chip, False)
 
         @pl.when(s != l)
         def _():
@@ -598,15 +536,16 @@
 def shards(latents, noise_levels, frame_lengths, kv_weight, mod_shift, mod_scale, mod_gate):
     dma = pltpu.SemaphoreType.DMA
     smem = pl.BlockSpec(memory_space=pltpu.SMEM)
-    vmem = pl.BlockSpec(memory_space=pltpu.VMEM)
     anywhere = pl.BlockSpec(memory_space=pl.ANY)
     wide = LAYERS - 1
     return pl.pallas_call(
         kernel,
         out_shape=jax.ShapeDtypeStruct((1, TOK, D), BF16),
-        in_specs=[smem, smem, vmem, anywhere, vmem, vmem, vmem],
+        in_specs=[smem, smem, anywhere, anywhere, anywhere, anywhere, anywhere],
         out_specs=anywhere,
         scratch_shapes=[
+            pltpu.VMEM((TOK, D), BF16),
+            pltpu.VMEM((3, 16, D), F32),
             pltpu.VMEM((LAYERS, BLOCKS, 2 * TOK, HEAD), BF16),
             pltpu.VMEM((wide, 2, SLICE, KVW), BF16),
             pltpu.VMEM((D, 2 * KVW), BF16),
@@ -616,18 +555,18 @@
             pltpu.VMEM((wide, SECTIONS, 8, HEAD), F32),
             pltpu.VMEM((8, D), F32),
             pltpu.VMEM((LAYERS, 8, SLICE), F32),
-            pltpu.VMEM((LAYERS, TOK, SLICE), BF16),
+            pltpu.VMEM((LAYERS + 1, TOK, SLICE), BF16),
             pltpu.VMEM((SLICE, HEAD), BF16),
             pltpu.VMEM((GRID * GRID, 16, 2 * TOK), BF16),
             pltpu.VMEM((8, SLICE), F32),
             pltpu.VMEM((PROWS, SLICE), F32),
             pltpu.VMEM((2, 2 * GRID * TOK, SLICE), F32),
             pltpu.VMEM((SECTIONS, 2 * TOK, HEAD), BF16),
-            dma((LAYERS, BLOCKS)), dma((LAYERS, 7)), dma((LAYERS, GRID, 3)), dma((LAYERS, GRID * GRID)),
+            dma((LAYERS, BLOCKS)), dma((LAYERS, GRID * GRID)), dma((LAYERS, GRID * GRID)),
             dma((wide,)), dma((SECTIONS,)), dma((2,)), dma((wide, GRID)), dma((wide, 3)), dma((wide, GRID)),
             dma((wide, 3)), dma((wide,)), dma((wide,)),
             dma((SECTIONS,)), dma((SECTIONS,)), dma((wide, SECTIONS)), dma((wide, SECTIONS)),
-            dma((wide, SECTIONS)), dma((wide, SECTIONS)), dma((SECTIONS,)), dma((LAYERS,)), dma((SECTIONS,)), dma((4,)),
+            dma((wide, SECTIONS)), dma((wide, SECTIONS)), dma((SECTIONS,)), dma((LAYERS,)), dma((SECTIONS,)), dma((4,)), dma((4,)),
         ],
         compiler_params=pltpu.CompilerParams(
             collective_id=0, has_side_effects=True, vmem_limit_bytes=56 * 1024 * 1024

time: 113 us -> 104 us (0.920)
  Pallas kernels: 110 us -> 102 us
    pallas_call x1, Pallas kernels: 110 us -> 102 us  [shards(): pl.pallas_call(kernel, out_shape=jax.ShapeDtypeStruct((1, TOK, D), BF16),...]
where the time goes in v4:
time: 104 us
  Pallas kernels  102 us (98%)
  local copies, waits for them, and re-layouts  2.06 us (2%)
    pallas_call x1, Pallas kernels, shards(): pl.pallas_call(kernel, out_shape=jax.ShapeDtypeStruct((1, TOK, D), BF16),...  102 us

profile of v4, /device:TPU:31, one launch (start us, length us, event | category | flops | bytes accessed | tf_op | source)
XLA Modules:
  0.0 104.0 jit_solution(11947669738930615175)
XLA Ops:
  0.0 102.0 %shard_map.73 = bf16[1,128,3072]{2,1,0:T(8,128)(2,1)} custom-call(s32[32]{0:T(128)} %levels.1, s32[32]{0:T(128)} %lengths.1, bf16[128,3072]{1,0:T(8,128)(2,1)} %latents_in.1, bf16[1,3072,1024]{2,1,0:T(8,128)(2,1)} %weight.1, f32[1,16,3072]{2,1,0:T(8,128)} %shift_in.1, f32[1,16,3072]{2,1,0:T(8,128)} %scale_in.1, f32[1,16,3072]{2,1,0:T(8,128)} %gate_in.1), custom_call_target="tpu_custom_call" | custom-call | tf_op jit(solution)/shard_map/pallas_call | solution.py:541
  102.0 2.1 %copy.9 = bf16[1,128,3072]{2,1,0:T(8,128)(2,1)} copy(bf16[1,128,3072]{2,1,0:T(8,128)(2,1)} %shard_map.73) | data formatting | bytes 1572864

commit v5 on v4

--- a/solution.py
+++ b/solution.py
@@ -138,6 +138,10 @@
         ref = wbuf.at[w, core, line_rows]
         return remote(ref, ref, s_w2s.at[w, d - 1], s_w2r.at[w, place_b], along_b(d), s)
 
+    def w2_piece(w, place, d):
+        ref = wbuf.at[w, core, pl.ds(pl.multiple_of((line_start + place) * PIECE, PIECE), PIECE)]
+        return remote(ref, ref, s_w2s.at[w, d - 1], s_w2r.at[w, place_b], along_b(d), s)
+
     def w3_copy(w):
         ref = wbuf.at[w, core]
         return remote(ref, ref, s_w3s.at[w], s_w3r.at[w], device(x, y, 1 - core), s)
@@ -148,16 +152,23 @@
             arrived(wbuf.at[w, core, piece_rows], s_wzr.at[w])
             for d in range(1, 4):
                 w1_copy(w, d).start()
+            if isinstance(w, int) and w == 0:
+                for d in range(1, 4):
+                    w2_piece(w, place_a, d).start()
 
     def w_step_b(w):
         @pl.when(s != w + 1)
         def _():
-            for d in range(1, 4):
+            for d in (1, 3, 2):
                 place = lax.rem(place_a + d, GRID)
                 rows = pl.ds(pl.multiple_of((line_start + place) * PIECE, PIECE), PIECE)
                 arrived(wbuf.at[w, core, rows], s_w1r.at[w, place])
-            for d in range(1, 4):
-                w2_copy(w, d).start()
+                if isinstance(w, int) and w == 0:
+                    for e in range(1, 4):
+                        w2_piece(w, place, e).start()
+            if not (isinstance(w, int) and w == 0):
+                for d in range(1, 4):
+                    w2_copy(w, d).start()
 
     def w_step_c(w):
         @pl.when(s != w + 1)
@@ -231,8 +242,7 @@
                 kv0[t, TOK:2 * TOK, :] = values
                 kv0_copy(t).start()
 
-    for w in range(LAYERS - 1):
-        w_step_a(w)
+    w_step_a(0)
 
     @pl.when(s != 0)
     def _():
@@ -346,6 +356,11 @@
         @pl.when((l == 0) & (s == 0))
         def _():
             w_step_b(0)
+
+        @pl.when(l == 0)
+        def _():
+            w_step_a(1)
+            w_step_a(2)
 
         mbuf[...] = jnp.full(mbuf.shape, -1e30, F32)
         accbuf[...] = jnp.zeros(accbuf.shape, F32)

time: 104 us -> 102 us (0.981)
  Pallas kernels: 102 us -> 100 us
    pallas_call x1, Pallas kernels: 102 us -> 100 us  [shards(): pl.pallas_call(kernel, out_shape=jax.ShapeDtypeStruct((1, TOK, D), BF16),...]
where the time goes in v5:
time: 102 us
  Pallas kernels  100 us (98%)
  local copies, waits for them, and re-layouts  2.06 us (2%)
    pallas_call x1, Pallas kernels, shards(): pl.pallas_call(kernel, out_shape=jax.ShapeDtypeStruct((1, TOK, D), BF16),...  100 us
    unnamed x1, local copies, waits for them, and re-layouts  2.06 us

profile of v5, /device:TPU:31, one launch (start us, length us, event | category | flops | bytes accessed | tf_op | source)
XLA Modules:
  0.0 102.1 jit_solution(8975638276719751015)
XLA Ops:
  0.0 100.1 %shard_map.73 = bf16[1,128,3072]{2,1,0:T(8,128)(2,1)} custom-call(s32[32]{0:T(128)} %levels.1, s32[32]{0:T(128)} %lengths.1, bf16[128,3072]{1,0:T(8,128)(2,1)} %latents_in.1, bf16[1,3072,1024]{2,1,0:T(8,128)(2,1)} %weight.1, f32[1,16,3072]{2,1,0:T(8,128)} %shift_in.1, f32[1,16,3072]{2,1,0:T(8,128)} %scale_in.1, f32[1,16,3072]{2,1,0:T(8,128)} %gate_in.1), custom_call_target="tpu_custom_call" | custom-call | tf_op jit(solution)/shard_map/pallas_call | solution.py:556
  100.1 2.1 %copy.9 = bf16[1,128,3072]{2,1,0:T(8,128)(2,1)} copy(bf16[1,128,3072]{2,1,0:T(8,128)(2,1)} %shard_map.73) | data formatting | bytes 1572864

commit v6 on v5

--- a/solution.py
+++ b/solution.py
@@ -39,9 +39,9 @@
 
 
 def kernel(levels, lengths, latents_in, weight, shift_in, scale_in, gate_in, out,
-           latents, tables, kvbuf, wbuf, w0buf, ybuf, psend, pbuf, statbuf, mods_own, mods, hbuf, qbuf, maskbuf, mbuf, accbuf, sbuf, kv0,
+           latents, tables, kvbuf, wbuf, w0buf, ybuf, psend, pbuf, statbuf, mods_own, mods, hbuf, qbuf, maskbuf, mbuf, accbuf, sbuf, kv0, rbuf,
            s_kvr, s_kvown, s_kvsib, s_wzr, s_wzs, s_wloc, s_w1r, s_w1s, s_w2r, s_w2s, s_w3r, s_w3s,
-           s_mods, s_modr, s_sts, s_str, s_ps, s_pr, s_kv0, s_outs, s_outr, s_w0, s_in):
+           s_mods, s_modr, s_sts, s_str, s_ps, s_pr, s_kv0, s_outs, s_outr, s_w0, s_in, s_half):
     c = lax.axis_index("stretch")
     s = lax.axis_index("section")
     core = lax.rem(c, 2)
@@ -339,6 +339,20 @@
 
     def out_remote(l):
         return remote(hbuf.at[l + 1], out.at[0, :, out_columns()], s_outs.at[l], s_outr.at[s], c, l)
+
+    last = LAYERS - 1
+    far = (last + 2) % SECTIONS
+    sides = ((last + 1) % SECTIONS, last - 1)
+    half = TOK // 2
+
+    def half_copy(i):
+        return remote(hbuf.at[LAYERS, pl.ds(i * half, half)], rbuf, s_half.at[i], s_half.at[2], c, sides[i])
+
+    def relay_copy(i):
+        return remote(rbuf, out.at[0, pl.ds(i * half, half), pl.ds(far * SLICE, SLICE)], s_half.at[3], s_outr.at[far], c, last)
+
+    def out_direct(l):
+        return (s != l) & ((l < last) | (s != far))
 
     def out_local(l):
         return pltpu.make_async_copy(hbuf.at[l + 1], out.at[0, :, out_columns()], s_outs.at[l])
@@ -489,10 +503,15 @@
             kvbuf[l + 1, c, 0:TOK, :] = keys
             kvbuf[l + 1, c, TOK:2 * TOK, :] = values
 
-        @pl.when(s != l)
+        @pl.when(out_direct(l))
         def _():
             out_remote(l).start()
 
+        @pl.when((l == last) & (s == far))
+        def _():
+            half_copy(0).start()
+            half_copy(1).start()
+
         @pl.when(s == l)
         def _():
             out_local(l).start()
@@ -500,13 +519,18 @@
         return carry
 
     lax.fori_loop(0, LAYERS, layer, 0)
+    for i in range(2):
+        @pl.when(s == sides[i])
+        def _(i=i):
+            arrived(rbuf, s_half.at[2])
+            relay_copy(i).start()
 
     def layer_sent(l, carry):
         own_copies(l, False)
 
         hand_over(l, 0, chip, False)
 
-        @pl.when(s != l)
+        @pl.when(out_direct(l))
         def _():
             out_remote(l).wait_send()
 
@@ -514,6 +538,15 @@
 
     lax.fori_loop(0, LAYERS, layer_sent, 0)
     out_local(s).wait()
+    for i in range(2):
+        @pl.when(s == sides[i])
+        def _(i=i):
+            relay_copy(i).wait_send()
+
+        @pl.when(s == far)
+        def _(i=i):
+            half_copy(i).wait_send()
+
     for d in range(1, 4):
         t = lax.rem(s + d, SECTIONS)
         mods_copy(t).wait_send()
@@ -577,11 +610,12 @@
             pltpu.VMEM((PROWS, SLICE), F32),
             pltpu.VMEM((2, 2 * GRID * TOK, SLICE), F32),
             pltpu.VMEM((SECTIONS, 2 * TOK, HEAD), BF16),
+            pltpu.VMEM((TOK // 2, SLICE), BF16),
             dma((LAYERS, BLOCKS)), dma((LAYERS, GRID * GRID)), dma((LAYERS, GRID * GRID)),
             dma((wide,)), dma((SECTIONS,)), dma((2,)), dma((wide, GRID)), dma((wide, 3)), dma((wide, GRID)),
             dma((wide, 3)), dma((wide,)), dma((wide,)),
             dma((SECTIONS,)), dma((SECTIONS,)), dma((wide, SECTIONS)), dma((wide, SECTIONS)),
-            dma((wide, SECTIONS)), dma((wide, SECTIONS)), dma((SECTIONS,)), dma((LAYERS,)), dma((SECTIONS,)), dma((4,)), dma((4,)),
+            dma((wide, SECTIONS)), dma((wide, SECTIONS)), dma((SECTIONS,)), dma((LAYERS,)), dma((SECTIONS,)), dma((4,)), dma((4,)), dma((4,)),
         ],
         compiler_params=pltpu.CompilerParams(
             collective_id=0, has_side_effects=True, vmem_limit_bytes=56 * 1024 * 1024

time: 102 us -> 100 us (0.980)
  Pallas kernels: 100 us -> 97.7 us
    pallas_call x1, Pallas kernels: 100 us -> 97.7 us  [shards(): pl.pallas_call(kernel, out_shape=jax.ShapeDtypeStruct((1, TOK, D), BF16),...]
where the time goes in v6:
time: 100 us; the launch traced here: 99.8 us
  Pallas kernels  97.7 us (98%)
  local copies, waits for them, and re-layouts  2.06 us (2%)
    pallas_call x1, Pallas kernels, shards(): pl.pallas_call(kernel, out_shape=jax.ShapeDtypeStruct((1, TOK, D), BF16),...  97.7 us
    unnamed x1, local copies, waits for them, and re-layouts  2.06 us

profile of v6, /device:TPU:31, one launch (start us, length us, event | category | flops | bytes accessed | tf_op | source)
XLA Modules:
  0.0 99.8 jit_solution(14629295415966642987)
XLA Ops:
  0.0 97.7 %shard_map.73 = bf16[1,128,3072]{2,1,0:T(8,128)(2,1)} custom-call(s32[32]{0:T(128)} %levels.1, s32[32]{0:T(128)} %lengths.1, bf16[128,3072]{1,0:T(8,128)(2,1)} %latents_in.1, bf16[1,3072,1024]{2,1,0:T(8,128)(2,1)} %weight.1, f32[1,16,3072]{2,1,0:T(8,128)} %shift_in.1, f32[1,16,3072]{2,1,0:T(8,128)} %scale_in.1, f32[1,16,3072]{2,1,0:T(8,128)} %gate_in.1), custom_call_target="tpu_custom_call" | custom-call | tf_op jit(solution)/shard_map/pallas_call | solution.py:589
  97.7 2.1 %copy.9 = bf16[1,128,3072]{2,1,0:T(8,128)(2,1)} copy(bf16[1,128,3072]{2,1,0:T(8,128)(2,1)} %shard_map.73) | data formatting | bytes 1572864

commit v7 on v6

--- a/solution.py
+++ b/solution.py
@@ -59,24 +59,24 @@
     def arrived(ref, sem):
         pltpu.make_async_copy(ref, ref, sem).wait()
 
+    barrier = pltpu.get_barrier_semaphore()
+    for d in range(1, SECTIONS):
+        pl.semaphore_signal(barrier, inc=1, device_id=(c, lax.rem(s + d, SECTIONS)), device_id_type=MESH)
+    pl.semaphore_signal(barrier, inc=1, device_id=(device(x, y, 1 - core), s), device_id_type=MESH)
+
+    def greet_chip(d, carry):
+        other = lax.rem(chip + d, GRID * GRID)
+        pl.semaphore_signal(barrier, inc=1, device_id=(2 * other + core, s), device_id_type=MESH)
+        return carry
+
+    lax.fori_loop(1, GRID * GRID, greet_chip, 0)
+
     inputs = [pltpu.make_async_copy(shift_in.at[0], tables.at[0], s_in.at[0]),
               pltpu.make_async_copy(scale_in.at[0], tables.at[1], s_in.at[1]),
               pltpu.make_async_copy(gate_in.at[0], tables.at[2], s_in.at[2]),
               pltpu.make_async_copy(latents_in, latents, s_in.at[3])]
     for copy in inputs:
         copy.start()
-
-    barrier = pltpu.get_barrier_semaphore()
-    for d in range(1, SECTIONS):
-        pl.semaphore_signal(barrier, inc=1, device_id=(c, lax.rem(s + d, SECTIONS)), device_id_type=MESH)
-    pl.semaphore_signal(barrier, inc=1, device_id=(device(x, y, 1 - core), s), device_id_type=MESH)
-
-    def greet_chip(d, carry):
-        other = lax.rem(chip + d, GRID * GRID)
-        pl.semaphore_signal(barrier, inc=1, device_id=(2 * other + core, s), device_id_type=MESH)
-        return carry
-
-    lax.fori_loop(1, GRID * GRID, greet_chip, 0)
 
     @pl.when(s == 0)
     def _():
@@ -208,11 +208,12 @@
         pl.semaphore_wait(barrier, SECTIONS + GRID * GRID - 1)
         for d in range(1, 4):
             t = lax.rem(s + d, SECTIONS)
-            mods_copy(t).start()
 
             @pl.when(s > 0)
             def _(t=t):
                 wz_copy(t).start()
+
+            mods_copy(t).start()
 
     pl.when(s > 0)(greet)
     inputs[3].wait()

time: 100 us -> 100 us (level)
  no operation moved by 1% of the time
where the time goes in v7:
time: 100 us; the launch traced here: 99.4 us
  Pallas kernels  97.3 us (97%)
  local copies, waits for them, and re-layouts  2.06 us (2%)
    pallas_call x1, Pallas kernels, shards(): pl.pallas_call(kernel, out_shape=jax.ShapeDtypeStruct((1, TOK, D), BF16),...  97.3 us
    unnamed x1, local copies, waits for them, and re-layouts  2.06 us

profile of v7, /device:TPU:31, one launch (start us, length us, event | category | flops | bytes accessed | tf_op | source)
XLA Modules:
  0.0 99.4 jit_solution(8046774264049919196)
XLA Ops:
  0.0 97.3 %shard_map.73 = bf16[1,128,3072]{2,1,0:T(8,128)(2,1)} custom-call(s32[32]{0:T(128)} %levels.1, s32[32]{0:T(128)} %lengths.1, bf16[128,3072]{1,0:T(8,128)(2,1)} %latents_in.1, bf16[1,3072,1024]{2,1,0:T(8,128)(2,1)} %weight.1, f32[1,16,3072]{2,1,0:T(8,128)} %shift_in.1, f32[1,16,3072]{2,1,0:T(8,128)} %scale_in.1, f32[1,16,3072]{2,1,0:T(8,128)} %gate_in.1), custom_call_target="tpu_custom_call" | custom-call | tf_op jit(solution)/shard_map/pallas_call | solution.py:590
  97.3 2.1 %copy.9 = bf16[1,128,3072]{2,1,0:T(8,128)(2,1)} copy(bf16[1,128,3072]{2,1,0:T(8,128)(2,1)} %shard_map.73) | data formatting | bytes 1572864
